TPU v7x, 128 devices: a whole 4x4x4 slice. The times are simulated.
128 devices in a mesh: dom: 32 (over y, x, core), rep: 4 (over z).
Axes of the slice: x: 4, y: 4, z: 4, core: 2. Of those that a mesh axis runs over, the one named last changes fastest.
Arguments:
- feature_grid: bfloat16 [32, 32, 32768], P('dom'), may hold values from -6 to 6
- fine_in: bfloat16 [32, 64, 32], P('dom'), may hold values from -1 to 1
- fine_mid: bfloat16 [32, 2, 64, 64], P('dom'), may hold values from -0.75 to 0.75
- fine_out: bfloat16 [32, 64], P('dom'), may hold values from -0.75 to 0.75
- prop_in: bfloat16 [32, 16, 32], P('dom'), may hold values from -1 to 1
- prop_out: bfloat16 [32, 16], P('dom'), may hold values from -1.5 to 1.5
- sample_cells: int32 [32, 4, 32, 2048], P('dom', 'rep'), may hold values from 0 to 31710, as said below
- sample_geometry: bfloat16 [4, 32, 4, 32, 2048], P(None, 'dom', 'rep'), may hold values from 0 to 1, as said below
- slot_ray: int32 [32, 4, 32, 32], P('dom', 'rep'), may hold values from 0 to 255, as said below
- slot_rank: int32 [32, 4, 32, 32], P('dom', 'rep'), may hold values from 0 to 31, as said below
- bucket_count: int32 [32, 4, 32], P('dom', 'rep'), may hold values from 1 to 32, as said below
Outputs:
- ray_loss: float32 [32, 4, 256], P('dom', 'rep')
- prop_in_grad: float32 [32, 16, 32], P('dom')
- prop_out_grad: float32 [32, 16], P('dom')
Inputs may be any that keep to these rules, and one draw needn't show every extreme that they name: `sample_cells`: each base cell's three coordinates lie in 0 to 30, so all eight corners are inside the grid. `sample_geometry`: rows 0 to 2 lie in 0 to 1; row 3 is positive. `slot_ray`: within one bucket the rays are distinct. `slot_rank`: live segments of one ray on one device have distinct ranks. `bucket_count`: the live slots of a bucket are its first ones; in every draw one partition receives full buckets from every device.
All inputs are finite; a program needn't handle non-finite values.
Results may differ from a plain program's by a relative error of at most 0.0024.
Values may be sent and summed in bfloat16 or wider, within the bound.
A program may use at most 192 MiB of HBM per device.

v0:
```python
import jax
import jax.numpy as jnp
from jax import lax
from jax.sharding import PartitionSpec as P

GR = 32
RAY_DEV = 256


distill_weight = 50.0
group_size = 4


def corner_table(grid_local, side):
    cell_major = jnp.transpose(grid_local)
    cell_total = cell_major.shape[0]
    reach = side * side + side + 1
    padded = jnp.concatenate(
        [cell_major, jnp.zeros((reach, cell_major.shape[1]), cell_major.dtype)], axis=0
    )
    pieces = []
    for corner in range(8):
        step_x = corner // 4
        step_y = corner // 2 % 2
        step_z = corner % 2
        start = (step_x * side + step_y) * side + step_z
        pieces.append(padded[start : start + cell_total])
    return jnp.concatenate(pieces, axis=1)


def interpolate(table, cell_index, geometry):
    offsets = geometry[:3].astype(jnp.float32)
    width = table.shape[1] // 8
    rows = jnp.take(table, cell_index, axis=0)
    summed = jnp.zeros((cell_index.shape[0], width), jnp.float32)
    for corner in range(8):
        step_x = corner // 4
        step_y = corner // 2 % 2
        step_z = corner % 2
        factor = (
            (offsets[0] if step_x else 1.0 - offsets[0])
            * (offsets[1] if step_y else 1.0 - offsets[1])
            * (offsets[2] if step_z else 1.0 - offsets[2])
        )
        summed = (
            summed
            + rows[:, corner * width : (corner + 1) * width].astype(jnp.float32) * factor[:, None]
        )
    return jnp.transpose(summed.astype(jnp.bfloat16))


def fine_density(fine_in, fine_mid, fine_out, features):
    hidden_units = jax.nn.relu(
        jnp.dot(fine_in, features, preferred_element_type=jnp.float32)
    ).astype(jnp.bfloat16)
    for layer_index in range(fine_mid.shape[0]):
        hidden_units = jax.nn.relu(
            jnp.dot(fine_mid[layer_index], hidden_units, preferred_element_type=jnp.float32)
        ).astype(jnp.bfloat16)
    return jax.nn.softplus(jnp.dot(fine_out, hidden_units, preferred_element_type=jnp.float32))


def proposal_parts(prop_in, prop_out, features):
    pre_hidden = jnp.dot(prop_in, features, preferred_element_type=jnp.float32)
    hidden_units = jax.nn.relu(pre_hidden).astype(jnp.bfloat16)
    logits = jnp.dot(prop_out, hidden_units, preferred_element_type=jnp.float32)
    return (pre_hidden, hidden_units, logits)


def proposal_grads(prop_in, prop_out, features, sigma_grad):
    pre_hidden, hidden_units, logits = proposal_parts(prop_in, prop_out, features)
    logit_grad = (sigma_grad * jax.nn.sigmoid(logits)).astype(jnp.bfloat16)
    out_grad = jnp.dot(hidden_units, logit_grad, preferred_element_type=jnp.float32)
    spread = prop_out[:, None].astype(jnp.float32) * logit_grad[None, :].astype(jnp.float32)
    hidden_grad = jnp.where(pre_hidden > 0, spread, jnp.float32(0.0)).astype(jnp.bfloat16)
    in_grad = lax.dot_general(
        hidden_grad, features, (((1,), (1,)), ((), ())), preferred_element_type=jnp.float32
    )
    return (in_grad, out_grad)


def absorbed(sigma, spacing):
    optical = sigma * spacing
    count = optical.shape[-2]
    lower = (jnp.arange(count)[:, None] >= jnp.arange(count)[None, :]).astype(jnp.float32)
    depth_sum = jnp.einsum("ij,pjc->pic", lower, optical, precision=lax.Precision.HIGHEST)
    return (jnp.exp(optical - depth_sum) - jnp.exp(-depth_sum), -depth_sum[..., -1, :])


def proposal_terms(sigma, fine_absorbed, spacing):
    prop_absorbed, log_prop = absorbed(sigma, spacing)
    return (
        jnp.sum(prop_absorbed * prop_absorbed, axis=-2),
        jnp.sum(prop_absorbed * fine_absorbed, axis=-2),
        log_prop,
    )


def segment_stats(prop_sigma, fine_sigma, spacing):
    fine_absorbed, log_fine = absorbed(fine_sigma, spacing)
    sum_aa, sum_ab, log_prop = proposal_terms(prop_sigma, fine_absorbed, spacing)
    sum_bb = jnp.sum(fine_absorbed * fine_absorbed, axis=-2)
    return (log_prop, log_fine, sum_aa, sum_ab, sum_bb)


def spread_sum(values, ray_table, rank_table, matrix):
    per_ray = lax.dot_general(
        ray_table,
        rank_table * values[None, :],
        (((1,), (1,)), ((), ())),
        precision=lax.Precision.HIGHEST,
    )
    per_ray = jnp.dot(per_ray, matrix, precision=lax.Precision.HIGHEST)
    spread = lax.dot_general(
        per_ray, ray_table, (((0,), (0,)), ((), ())), precision=lax.Precision.HIGHEST
    )
    return jnp.sum(spread * rank_table, axis=0)


def ray_side(log_prop, log_fine, sum_aa, sum_ab, sum_bb, ray_ids, rank_ids, counts):
    part_count, capacity = ray_ids.shape
    live_mask = (jnp.arange(capacity)[None, :] < counts[:, None]).astype(jnp.float32).reshape(-1)
    ray_flat = ray_ids.reshape(-1)
    rank_flat = rank_ids.reshape(-1)
    ray_table = (jnp.arange(RAY_DEV)[:, None] == ray_flat[None, :]).astype(jnp.float32)
    rank_table = (jnp.arange(part_count)[:, None] == rank_flat[None, :]).astype(jnp.float32)
    later = (jnp.arange(part_count)[:, None] < jnp.arange(part_count)[None, :]).astype(jnp.float32)
    entry_prop = (
        jnp.exp(spread_sum(log_prop.reshape(-1) * live_mask, ray_table, rank_table, later))
        * live_mask
    )
    entry_fine = (
        jnp.exp(spread_sum(log_fine.reshape(-1) * live_mask, ray_table, rank_table, later))
        * live_mask
    )
    flat_aa = sum_aa.reshape(-1)
    flat_ab = sum_ab.reshape(-1)
    flat_bb = sum_bb.reshape(-1)
    seg_loss = (
        entry_prop * entry_prop * flat_aa
        - 2.0 * entry_prop * entry_fine * flat_ab
        + entry_fine * entry_fine * flat_bb
    )
    slot_grad = distill_weight * (entry_prop * flat_aa - entry_fine * flat_ab) * entry_prop
    carried = spread_sum(slot_grad, ray_table, rank_table, later.T) * live_mask
    ray_loss = 0.5 * distill_weight * jnp.dot(ray_table, seg_loss, precision=lax.Precision.HIGHEST)
    coef_aa = 0.5 * distill_weight * entry_prop * entry_prop
    coef_ab = -distill_weight * entry_prop * entry_fine
    return (jnp.stack([coef_aa, coef_ab, carried]).reshape(3, part_count, capacity), ray_loss)


def on_device(
    feature_grid,
    fine_in,
    fine_mid,
    fine_out,
    prop_in,
    prop_out,
    sample_cells,
    sample_geometry,
    slot_ray,
    slot_rank,
    bucket_count,
):
    part_count = lax.axis_size("dom")
    capacity = slot_ray.shape[3]
    bucket_width = sample_cells.shape[3]
    per_slot = bucket_width // capacity
    groups = part_count // group_size
    group_span = group_size * bucket_width
    arrived = lax.all_to_all(sample_geometry, "dom", split_axis=3, concat_axis=3, tiled=True)
    cell_groups = sample_cells.reshape(groups, group_span)
    geometry_groups = jnp.moveaxis(arrived.reshape(4, groups, group_span), 1, 0)
    table = corner_table(feature_grid[0], GR)

    def forward_group(packed):
        cell_index, geometry = packed
        features = interpolate(table, cell_index, geometry)
        fine_sigma = fine_density(fine_in[0], fine_mid[0], fine_out[0], features)
        prop_sigma = jax.nn.softplus(proposal_parts(prop_in[0], prop_out[0], features)[2])
        return (features, prop_sigma, fine_sigma)

    features_all, prop_sigma, fine_sigma = lax.map(forward_group, (cell_groups, geometry_groups))
    ray_ids = slot_ray[0, 0]
    rank_ids = slot_rank[0, 0]
    counts = bucket_count[0, 0]
    both_sigma = jnp.stack([prop_sigma, fine_sigma]).reshape(2, 1, 1, part_count, bucket_width)
    returned = lax.all_to_all(both_sigma, "dom", split_axis=3, concat_axis=3, tiled=True)
    own_spacing = (
        sample_geometry[3, 0, 0].astype(jnp.float32).reshape(part_count, per_slot, capacity)
    )
    ray_prop = returned[0, 0, 0].reshape(part_count, per_slot, capacity)
    ray_fine = returned[1, 0, 0].reshape(part_count, per_slot, capacity)
    stats = segment_stats(ray_prop, ray_fine, own_spacing)
    factors, ray_loss = ray_side(
        stats[0], stats[1], stats[2], stats[3], stats[4], ray_ids, rank_ids, counts
    )
    fine_absorbed = absorbed(ray_fine, own_spacing)[0]
    terms_value, pullback = jax.vjp(
        lambda sigma: proposal_terms(sigma, fine_absorbed, own_spacing), ray_prop
    )
    sigma_grad = pullback((factors[0], factors[1], factors[2]))[0]
    owner_grad = lax.all_to_all(
        sigma_grad.reshape(1, 1, part_count, bucket_width),
        "dom",
        split_axis=2,
        concat_axis=2,
        tiled=True,
    )
    sigma_grad_owner = owner_grad.reshape(groups, group_span)

    def backward_group(running, packed):
        features, sigma_block = packed
        in_grad, out_grad = proposal_grads(prop_in[0], prop_out[0], features, sigma_block)
        return ((running[0] + in_grad, running[1] + out_grad), None)

    initial = (
        jnp.zeros(prop_in.shape[1:], jnp.float32),
        jnp.zeros(prop_out.shape[1:], jnp.float32),
    )
    totals, unused = lax.scan(backward_group, initial, (features_all, sigma_grad_owner))
    in_sum, out_sum = lax.psum((totals[0], totals[1]), "rep")
    return (ray_loss.reshape(1, 1, -1), in_sum[None], out_sum[None])


def solution(mesh):
    return jax.shard_map(
        on_device,
        mesh=mesh,
        in_specs=(
            P("dom", None, None),
            P("dom", None, None),
            P("dom", None, None, None),
            P("dom", None),
            P("dom", None, None),
            P("dom", None),
            P("dom", "rep", None, None),
            P(None, "dom", "rep", None, None),
            P("dom", "rep", None, None),
            P("dom", "rep", None, None),
            P("dom", "rep", None),
        ),
        out_specs=(P("dom", "rep", None), P("dom", None, None), P("dom", None)),
        check_vma=False,
    )
```

profile of v0, /device:TPU:0, one launch (start us, length us, event | category | flops | bytes accessed | tf_op | source)
XLA Modules:
  0.0 645.0 jit_solution(16933003515552783970)
XLA Ops:
  2.9 7.4 %all-to-all-start = ((bf16[4,1,1,32,2048]{4,0,2,1,3:T(4,128)(2,1)}), bf16[4,1,1,32,2048]{4,0,2,1,3:T(4,128)(2,1)S(1)}, u32[]{:S(2)}, u32[]{:S(2)}) async-start(bf16[4,1,1,32,2048]{4,0,2,1,3:T(4,128)(2,1)} %copy.54), calls=%async_computation | async-start | bytes 1048576 | tf_op jit(solution)/shard_map/all_to_all | solution.py:171
  10.3 7.4 %copy.53 = bf16[1,32,32768]{1,2,0:T(8,128)(2,1)} copy(bf16[1,32,32768]{2,1,0:T(8,128)(2,1)} %param.15) | data formatting | bytes 4194304 | tf_op args[0]
  17.6 47.0 %pad_slice_fusion = (bf16[32768,32]{1,0:T(8,128)(2,1)}, bf16[32768,32]{1,0:T(8,128)(2,1)}, bf16[32768,32]{1,0:T(8,128)(2,1)}, bf16[32768,32]{1,0:T(8,128)(2,1)},...) fusion(bf16[32768,32]{1,0:T(8,128)(2,1)} %bitcast.193), kind=kLoop, calls=%fused_computation.76 | loop fusion | bytes 16777216 | tf_op jit(solution)/shard_map/slice | solution.py:27
  64.9 63.3 %concatenate.8 = bf16[32768,256]{1,0:T(8,128)(2,1)} concatenate(bf16[32768,32]{1,0:T(8,128)(2,1)} %bitcast.194, bf16[32768,32]{1,0:T(8,128)(2,1)} %get-tuple-element.279, bf16[32768,32]{1,0:T(8,128)(2,1)} %get-tuple-element.274, bf16[32768,32]{1,0:T(8,128)(2,1)} %get-tuple-element.275, bf16[32768,32]{1,0:T(8,128)(2,1)} %get-tuple-element.276, ...), dimensions={1} | concatenate | bytes 33554432 | tf_op jit(solution)/shard_map/concatenate | solution.py:28
  129.4 431.4 %while.27 = (s32[]{:T(128)}, bf16[8,32,8192]{2,1,0:T(8,128)(2,1)}, f32[8,8192]{1,0:T(8,128)S(1)}, f32[8,8192]{1,0:T(8,128)S(1)}, s32[8,8192]{1,0:T(8,128)S(1)}, ...) while((s32[]{:T(128)}, bf16[8,32,8192]{2,1,0:T(8,128)(2,1)}, ...), condition=%wide.region_1.2_spmd, body=%wide.region_0.1_spmd.sunk | while | flops 189595648 | bytes 35137716 | solution.py:183
  129.6 38.8 %gather_fusion = bf16[8192,256]{1,0:T(8,128)(2,1)} fusion(bf16[32768,256]{1,0:T(8,128)(2,1)} %get-tuple-element.472, s32[8192]{0:T(1024)S(1)} %broadcast_clamp_fusion.2), kind=kCustom, calls=%fused_computation.clone.1 | custom fusion | bytes 8421376 | tf_op jit(solution)/shard_map/while/body/eval_jaxpr/jit(_take)/gather | solution.py:34
  168.4 6.4 copy.66
  183.5 38.8 %gather_fusion = bf16[8192,256]{1,0:T(8,128)(2,1)} fusion(bf16[32768,256]{1,0:T(8,128)(2,1)} %get-tuple-element.472, s32[8192]{0:T(1024)S(1)} %broadcast_clamp_fusion.2), kind=kCustom, calls=%fused_computation.clone.1 | custom fusion | bytes 8421376 | tf_op jit(solution)/shard_map/while/body/eval_jaxpr/jit(_take)/gather | solution.py:34
  222.3 6.4 copy.66
  237.4 38.8 %gather_fusion = bf16[8192,256]{1,0:T(8,128)(2,1)} fusion(bf16[32768,256]{1,0:T(8,128)(2,1)} %get-tuple-element.472, s32[8192]{0:T(1024)S(1)} %broadcast_clamp_fusion.2), kind=kCustom, calls=%fused_computation.clone.1 | custom fusion | bytes 8421376 | tf_op jit(solution)/shard_map/while/body/eval_jaxpr/jit(_take)/gather | solution.py:34
  291.3 38.8 %gather_fusion = bf16[8192,256]{1,0:T(8,128)(2,1)} fusion(bf16[32768,256]{1,0:T(8,128)(2,1)} %get-tuple-element.472, s32[8192]{0:T(1024)S(1)} %broadcast_clamp_fusion.2), kind=kCustom, calls=%fused_computation.clone.1 | custom fusion | bytes 8421376 | tf_op jit(solution)/shard_map/while/body/eval_jaxpr/jit(_take)/gather | solution.py:34
  330.1 6.4 copy.66
  345.2 38.8 %gather_fusion = bf16[8192,256]{1,0:T(8,128)(2,1)} fusion(bf16[32768,256]{1,0:T(8,128)(2,1)} %get-tuple-element.472, s32[8192]{0:T(1024)S(1)} %broadcast_clamp_fusion.2), kind=kCustom, calls=%fused_computation.clone.1 | custom fusion | bytes 8421376 | tf_op jit(solution)/shard_map/while/body/eval_jaxpr/jit(_take)/gather | solution.py:34
  399.1 38.8 %gather_fusion = bf16[8192,256]{1,0:T(8,128)(2,1)} fusion(bf16[32768,256]{1,0:T(8,128)(2,1)} %get-tuple-element.472, s32[8192]{0:T(1024)S(1)} %broadcast_clamp_fusion.2), kind=kCustom, calls=%fused_computation.clone.1 | custom fusion | bytes 8421376 | tf_op jit(solution)/shard_map/while/body/eval_jaxpr/jit(_take)/gather | solution.py:34
  437.9 6.4 copy.66
  453.1 38.8 %gather_fusion = bf16[8192,256]{1,0:T(8,128)(2,1)} fusion(bf16[32768,256]{1,0:T(8,128)(2,1)} %get-tuple-element.472, s32[8192]{0:T(1024)S(1)} %broadcast_clamp_fusion.2), kind=kCustom, calls=%fused_computation.clone.1 | custom fusion | bytes 8421376 | tf_op jit(solution)/shard_map/while/body/eval_jaxpr/jit(_take)/gather | solution.py:34
  491.9 6.4 copy.66
  506.9 38.8 %gather_fusion = bf16[8192,256]{1,0:T(8,128)(2,1)} fusion(bf16[32768,256]{1,0:T(8,128)(2,1)} %get-tuple-element.472, s32[8192]{0:T(1024)S(1)} %broadcast_clamp_fusion.2), kind=kCustom, calls=%fused_computation.clone.1 | custom fusion | bytes 8421376 | tf_op jit(solution)/shard_map/while/body/eval_jaxpr/jit(_take)/gather | solution.py:34
  545.7 6.4 copy.66
  562.9 7.4 %all-to-all-start.1 = ((f32[2,1,1,32,2048]{4,2,1,0,3:T(1,128)}), f32[2,1,1,32,2048]{4,2,1,0,3:T(1,128)S(1)}, u32[]{:S(2)}, u32[]{:S(2)}) async-start(f32[2,1,1,32,2048]{4,2,1,0,3:T(1,128)} %pad_maximum_fusion), calls=%async_computation.1 | async-start | bytes 1048576 | tf_op jit(solution)/shard_map/all_to_all | solution.py:188
  572.2 9.8 %all-to-all-done.1 = f32[2,1,1,32,2048]{4,2,1,0,3:T(1,128)S(1)} async-done(((f32[2,1,1,32,2048]{4,2,1,0,3:T(1,128)}), f32[2,1,1,32,2048]{4,2,1,0,3:T(1,128)S(1)}, u32[]{:S(2)}, u32[]{:S(2)}) %all-to-all-start.1) | async-done | bytes 524320 | tf_op jit(solution)/shard_map/all_to_all | solution.py:188
  599.0 7.8 %all-to-all-done.2 = f32[1,1,32,2048]{3,1,0,2:T(1,128)S(1)} async-done(((f32[1,1,32,2048]{3,1,0,2:T(1,128)}), f32[1,1,32,2048]{3,1,0,2:T(1,128)S(1)}, u32[]{:S(2)}, u32[]{:S(2)}) %all-to-all-start.2) | async-done | bytes 262176 | tf_op jit(solution)/shard_map/all_to_all | solution.py:203
  607.5 24.9 %while.28 = (s32[]{:T(128)}, f32[16,32]{1,0:T(8,128)S(1)}, f32[16]{0:T(128)S(1)}, bf16[8,32,8192]{2,1,0:T(8,128)(2,1)}, bf16[1,16,32]{2,1,0:T(8,128)(2,1)S(1)}, ...) while((s32[]{:T(128)}, f32[16,32]{1,0:T(8,128)S(1)}, ...), condition=%wide.region_9.10_spmd.clone, body=%wide.region_8.9_spmd.clone.sunk | while | flops 18400308 | bytes 3447212 | solution.py:221
  632.4 12.6 %all-reduce.2 = (f32[1,16,32]{2,1,0:T(8,128)}, f32[1,16]{1,0:T(1,128)}) all-reduce(f32[1,16,32]{2,1,0:T(8,128)S(1)} %bitcast.207, f32[1,16]{1,0:T(1,128)S(1)} %bitcast.208), channel_id=1, replica_groups=mesh['dom'=32,'rep'=4] {'rep'}, use_global_device_ids=true, to_apply=%region_10.11 | all-reduce | flops 528 | bytes 4224 | tf_op jit(solution)/shard_map/psum | solution.py:222
  (263 shorter events, 131.3 us)
Async XLA Ops:
  2.9 125.3 %all-to-all-start = ((bf16[4,1,1,32,2048]{4,0,2,1,3:T(4,128)(2,1)}), bf16[4,1,1,32,2048]{4,0,2,1,3:T(4,128)(2,1)S(1)}, u32[]{:S(2)}, u32[]{:S(2)}) async-start(bf16[4,1,1,32,2048]{4,0,2,1,3:T(4,128)(2,1)} %copy.54), calls=%async_computation | async-start | bytes 1048576 | tf_op jit(solution)/shard_map/all_to_all | solution.py:171
  17.6 47.1 %copy-start.1 = (s32[1,1,32,2048]{3,2,1,0:T(8,128)S(1)}, s32[1,1,32,2048]{3,2,1,0:T(8,128)}, u32[]{:S(2)}) copy-start(s32[1,1,32,2048]{3,2,1,0:T(8,128)} %param.21) | copy-start | bytes 786436
  64.8 64.5 %copy-start = (bf16[1,16,32]{2,1,0:T(8,128)(2,1)S(1)}, bf16[1,16,32]{2,1,0:T(8,128)(2,1)}, u32[]{:S(2)}) copy-start(bf16[1,16,32]{2,1,0:T(8,128)(2,1)} %param.19) | copy-start | bytes 3076
  64.8 64.5 %copy-start.2 = (bf16[1,16]{1,0:T(2,128)(2,1)S(1)}, bf16[1,16]{1,0:T(2,128)(2,1)}, u32[]{:S(2)}) copy-start(bf16[1,16]{1,0:T(2,128)(2,1)} %param.20) | copy-start | bytes 100
  64.9 64.5 %copy-start.6 = (bf16[1,2,64,64]{3,2,1,0:T(8,128)(2,1)S(1)}, bf16[1,2,64,64]{3,2,1,0:T(8,128)(2,1)}, u32[]{:S(2)}) copy-start(bf16[1,2,64,64]{3,2,1,0:T(8,128)(2,1)} %param.17) | copy-start | bytes 49156
  64.9 64.5 %copy-start.7 = (bf16[1,64,32]{1,2,0:T(8,128)(2,1)S(1)}, bf16[1,64,32]{1,2,0:T(8,128)(2,1)}, u32[]{:S(2)}) copy-start(bf16[1,64,32]{1,2,0:T(8,128)(2,1)} %param.16) | copy-start | bytes 12292
  64.9 64.5 %copy-start.8 = (bf16[1,64]{1,0:T(2,128)(2,1)S(1)}, bf16[1,64]{1,0:T(2,128)(2,1)}, u32[]{:S(2)}) copy-start(bf16[1,64]{1,0:T(2,128)(2,1)} %param.18) | copy-start | bytes 388
  560.8 11.1 %copy-start.5 = (s32[1,1,32]{2,1,0:T(1,128)S(1)}, s32[1,1,32]{2,1,0:T(1,128)}, u32[]{:S(2)}) copy-start(s32[1,1,32]{2,1,0:T(1,128)} %param.25) | copy-start | bytes 388
  560.8 11.2 %copy-start.3 = (s32[1,1,32,32]{3,2,1,0:T(8,128)S(1)}, s32[1,1,32,32]{3,2,1,0:T(8,128)}, u32[]{:S(2)}) copy-start(s32[1,1,32,32]{3,2,1,0:T(8,128)} %param.23) | copy-start | bytes 12292
  560.8 11.3 %copy-start.4 = (s32[1,1,32,32]{3,2,1,0:T(8,128)S(1)}, s32[1,1,32,32]{3,2,1,0:T(8,128)}, u32[]{:S(2)}) copy-start(s32[1,1,32,32]{3,2,1,0:T(8,128)} %param.24) | copy-start | bytes 12292
  562.9 19.2 %all-to-all-start.1 = ((f32[2,1,1,32,2048]{4,2,1,0,3:T(1,128)}), f32[2,1,1,32,2048]{4,2,1,0,3:T(1,128)S(1)}, u32[]{:S(2)}, u32[]{:S(2)}) async-start(f32[2,1,1,32,2048]{4,2,1,0,3:T(1,128)} %pad_maximum_fusion), calls=%async_computation.1 | async-start | bytes 1048576 | tf_op jit(solution)/shard_map/all_to_all | solution.py:188
  594.0 12.8 %all-to-all-start.2 = ((f32[1,1,32,2048]{3,1,0,2:T(1,128)}), f32[1,1,32,2048]{3,1,0,2:T(1,128)S(1)}, u32[]{:S(2)}, u32[]{:S(2)}) async-start(f32[1,1,32,2048]{3,1,0,2:T(1,128)} %reshape.363), calls=%async_computation.2 | async-start | bytes 524288 | tf_op jit(solution)/shard_map/all_to_all | solution.py:203
where the time goes:
time: 651 us; the launch traced here: 645 us
  local copies, waits for them, and re-layouts  493 us (76%)
  matrix products  60.8 us (9%)
  other arithmetic  40.3 us (6%)
  starting transfers between devices  18.7 us (3%)
  waiting for transfers between devices  17.6 us (3%)
  blocking collectives  12.6 us (2%)
    gather x16, local copies, waits for them, and re-layouts, interpolate(): rows = jnp.take(table, cell_index, axis=0)  361 us
    concatenate x1, local copies, waits for them, and re-layouts, corner_table(): return jnp.concatenate(pieces, axis=1)  63.3 us
    slice x1, local copies, waits for them, and re-layouts, corner_table(): pieces.append(padded[start:start + cell_total])  47 us
    select_n x16, other arithmetic, interpolate(): rows = jnp.take(table, cell_index, axis=0)  21.4 us
    dot_general x8, matrix products, fine_density(): jnp.dot(fine_out, hidden_units, preferred_element_type=jnp.float32)  14.1 us
    dot_general x8, matrix products, fine_density(): jnp.dot(fine_mid[layer_index], hidden_units, preferred_element_type=jnp.f...  14 us
    dynamic_update_slice x8, other arithmetic, on_device(): lax.map(forward_group, (cell_groups, geometry_groups))  13.2 us
  transfers between devices with their start and end apart: 3, of which 2 were waited for; matrix products, arithmetic and copies ran while one was open for 19% of the time, Pallas kernels for 0%

commit v1 on v0

v1 whole, which is shorter than its diff:
```python
import functools

import jax
import jax.numpy as jnp
from jax import lax
from jax.experimental import pallas as pl
from jax.experimental.pallas import tpu as pltpu
from jax.sharding import PartitionSpec as P

GR = 32
RAY_DEV = 256
TILE = 512

distill_weight = 50.0
f32 = jnp.float32
bf16 = jnp.bfloat16
LANES_BOTH = (((1,), (1,)), ((), ()))


def softplus(x):
    return jnp.maximum(x, 0.0) + jnp.log1p(jnp.exp(-jnp.abs(x)))


def group_total(x):
    once = x + pltpu.roll(x, 32, 1)
    return once + pltpu.roll(once, 64, 1)


def scan_segment(x, rows, forward):
    lane = lax.broadcasted_iota(jnp.int32, x.shape, 1)
    row = lax.broadcasted_iota(jnp.int32, x.shape, 0) % rows
    height = x.shape[0]

    def moved(value, step, axis):
        size = height if axis == 0 else 128
        return pltpu.roll(value, step if forward else size - step, axis)

    within = x
    for step in (32, 64):
        keep = lane >= step if forward else lane < 128 - step
        within = within + jnp.where(keep, moved(within, step, 1), 0.0)
    total = group_total(x)
    running = total
    step = 1
    while step < rows:
        keep = row >= step if forward else row < rows - step
        running = running + jnp.where(keep, moved(running, step, 0), 0.0)
        step *= 2
    edge = row >= 1 if forward else row < rows - 1
    return within + jnp.where(edge, moved(running, 1, 0), 0.0), total


def owner_kernel(
    cells_ref, geom_ref, grid_ref, fine_in_ref, fine_mid_ref, fine_out_ref, prop_in_ref, prop_out_ref,
    kept_ref, back_ref, stats_ref,
    table, even0, even1, odd0, odd1, geo, fine_logit, prop_logit, spacing,
):
    sources, width = cells_ref.shape
    tiles_per = width // TILE
    tile_total = sources * tiles_per
    cell_blocks = grid_ref.shape[1] // 128
    rows_per = width // 128

    geo[...] = geom_ref[...].astype(f32)
    lane = lax.broadcasted_iota(jnp.int32, (GR, 128), 1)

    def build(block, carry):
        here = grid_ref[:, pl.ds(pl.multiple_of(block * 128, 128), 128)].astype(f32)
        after = jnp.minimum(block + 1, cell_blocks - 1)
        there = grid_ref[:, pl.ds(pl.multiple_of(after * 128, 128), 128)].astype(f32)
        pieces = [here]
        for shift in (1, GR, GR + 1):
            pieces.append(
                jnp.where(
                    lane < 128 - shift,
                    pltpu.roll(here, 128 - shift, 1),
                    pltpu.roll(there, 128 - shift, 1),
                )
            )
        table[pl.ds(pl.multiple_of(block * 128, 128), 128), :] = jnp.transpose(
            jnp.concatenate(pieces, axis=0)
        )
        return carry

    lax.fori_loop(0, cell_blocks, build, 0, unroll=2)

    first = jnp.concatenate([fine_in_ref[...], prop_in_ref[...]], axis=0)
    hidden = fine_in_ref.shape[0]
    eye = (
        lax.broadcasted_iota(jnp.int32, (256, 256), 0)
        == lax.broadcasted_iota(jnp.int32, (256, 256), 1)
    ).astype(f32).astype(bf16)

    def gather(tile, low, high):
        source = tile // tiles_per
        base = (tile % tiles_per) * TILE
        for j in range(TILE):
            cell = cells_ref[source, base + j]
            low[pl.ds(j, 1), :] = table[pl.ds(cell, 1), :]
            high[pl.ds(j, 1), :] = table[pl.ds(cell + GR * GR, 1), :]

    def evaluate(tile, low, high):
        source = tile // tiles_per
        lanes = pl.ds(pl.multiple_of((tile % tiles_per) * TILE, TILE), TILE)
        rows = jnp.concatenate([low[...], high[...]], axis=1).astype(bf16)
        turned = lax.dot_general(eye, rows, LANES_BOTH, preferred_element_type=f32)
        offsets = [geo[axis, pl.ds(source, 1), lanes] for axis in range(3)]
        factors = [[1.0 - value, value] for value in offsets]
        summed = jnp.zeros((32, TILE), f32)
        for corner in range(8):
            factor = (
                factors[0][corner // 4] * factors[1][corner // 2 % 2] * factors[2][corner % 2]
            )
            summed = summed + turned[corner * 32 : (corner + 1) * 32] * factor
        features = summed.astype(bf16)
        both = jnp.maximum(jnp.dot(first, features, preferred_element_type=f32), 0.0).astype(bf16)
        prop_hidden = both[hidden:]
        fine_hidden = both[:hidden]
        kept_ref[source, pl.ds(0, 32), lanes] = features
        kept_ref[source, pl.ds(32, 16), lanes] = prop_hidden
        for layer in range(fine_mid_ref.shape[0]):
            fine_hidden = jnp.maximum(
                jnp.dot(fine_mid_ref[layer], fine_hidden, preferred_element_type=f32), 0.0
            ).astype(bf16)
        fine = jnp.dot(fine_out_ref[...], fine_hidden, preferred_element_type=f32)
        prop = jnp.dot(prop_out_ref[...], prop_hidden, preferred_element_type=f32)
        step = geo[3, pl.ds(source, 1), lanes]
        for part in range(TILE // 128):
            row = pl.ds(tile * (TILE // 128) + part, 1)
            cut = slice(part * 128, (part + 1) * 128)
            fine_logit[row, :] = fine[:, cut]
            prop_logit[row, :] = prop[:, cut]
            spacing[row, :] = step[:, cut]

    gather(0, even0, even1)

    def pair(index, carry):
        tile = index * 2
        gather(tile + 1, odd0, odd1)
        evaluate(tile, even0, even1)
        gather(jnp.minimum(tile + 2, tile_total - 1), even0, even1)
        evaluate(tile + 1, odd0, odd1)
        return carry

    lax.fori_loop(0, tile_total // 2, pair, 0)

    gap = spacing[...]
    prop_raw = prop_logit[...]
    optical = softplus(prop_raw) * gap
    depth, prop_total = scan_segment(optical, rows_per, True)
    before = jnp.exp(optical - depth)
    prop_taken = before - jnp.exp(-depth)
    back_ref[0] = prop_taken
    back_ref[1] = before
    back_ref[2] = gap * jax.nn.sigmoid(prop_raw)
    fine_optical = softplus(fine_logit[...]) * gap
    fine_depth, fine_total = scan_segment(fine_optical, rows_per, True)
    fine_taken = jnp.exp(fine_optical - fine_depth) - jnp.exp(-fine_depth)
    back_ref[3] = fine_taken

    def per_segment(value, totalled):
        over_rows = jnp.sum(value.reshape(sources, rows_per, 128), axis=1)
        return over_rows if totalled else group_total(over_rows)

    sum_aa = per_segment(prop_taken * prop_taken, False)
    sum_ab = per_segment(prop_taken * fine_taken, False)
    sum_bb = per_segment(fine_taken * fine_taken, False)
    log_prop = -per_segment(prop_total, True)
    log_fine = -per_segment(fine_total, True)
    part = lax.broadcasted_iota(jnp.int32, (sources, 128), 1) // 32
    stats_ref[:, pl.ds(0, 128)] = jnp.where(
        part == 0, sum_aa, jnp.where(part == 1, sum_ab, jnp.where(part == 2, sum_bb, log_prop))
    )
    stats_ref[:, pl.ds(128, 128)] = log_fine


def split_three(value):
    high = value.astype(bf16)
    rest = value - high.astype(f32)
    middle = rest.astype(bf16)
    low = (rest - middle.astype(f32)).astype(bf16)
    return [high, middle, low]


def ray_kernel(stats_ref, ray_row_ref, rank_row_ref, live_ref, ray_col_ref, rank_col_ref, factor_ref, loss_ref, ahead):
    slots = stats_ref.shape[1]
    key_row = ray_row_ref[...] * 64 + rank_row_ref[...]
    rank_row = rank_row_ref[...]
    live = live_ref[...]
    sum_aa, sum_ab, sum_bb, log_prop, log_fine = (stats_ref[pl.ds(i, 1), :] for i in range(5))

    def stacked(values):
        pieces = [piece.astype(f32) for value in values for piece in split_three(value)]
        pieces += [jnp.zeros_like(pieces[0])] * (8 - len(pieces))
        return jnp.concatenate(pieces, axis=0).astype(bf16)

    logs = stacked([log_prop * live, log_fine * live])
    reached = jnp.zeros((8, slots), f32)
    for chunk in range(slots // 128):
        rows = pl.ds(chunk * 128, 128)
        gap = key_row - (ray_col_ref[rows, :] * 64 + rank_col_ref[rows, :])
        mask = jnp.where((gap > 0) & (gap <= rank_row), 1.0, 0.0).astype(bf16)
        ahead[rows, :] = mask
        reached = reached + jnp.dot(
            logs[:, chunk * 128 : (chunk + 1) * 128], mask, preferred_element_type=f32
        )
    entry_prop = jnp.exp(reached[0:1] + reached[1:2] + reached[2:3]) * live
    entry_fine = jnp.exp(reached[3:4] + reached[4:5] + reached[5:6]) * live
    seg_loss = (
        entry_prop * entry_prop * sum_aa
        - 2.0 * entry_prop * entry_fine * sum_ab
        + entry_fine * entry_fine * sum_bb
    )
    slot_grad = distill_weight * (entry_prop * sum_aa - entry_fine * sum_ab) * entry_prop
    carried = lax.dot_general(
        stacked([slot_grad]), ahead[...], LANES_BOTH, preferred_element_type=f32
    )
    factor_ref[pl.ds(0, 1), :] = 0.5 * distill_weight * entry_prop * entry_prop
    factor_ref[pl.ds(1, 1), :] = -distill_weight * entry_prop * entry_fine
    factor_ref[pl.ds(2, 1), :] = (carried[0:1] + carried[1:2] + carried[2:3]) * live
    factor_ref[pl.ds(3, 1), :] = jnp.zeros_like(live)
    losses = stacked([seg_loss])
    ray_loss = jnp.zeros((8, RAY_DEV), f32)
    ray_ids = lax.broadcasted_iota(jnp.int32, (128, RAY_DEV), 1)
    for chunk in range(slots // 128):
        mask = jnp.where(ray_col_ref[pl.ds(chunk * 128, 128), :] == ray_ids, 1.0, 0.0).astype(bf16)
        ray_loss = ray_loss + jnp.dot(
            losses[:, chunk * 128 : (chunk + 1) * 128], mask, preferred_element_type=f32
        )
    loss_ref[...] = 0.5 * distill_weight * (ray_loss[0:1] + ray_loss[1:2] + ray_loss[2:3])


def backward_kernel(factor_ref, back_ref, kept_ref, prop_out_ref, in_ref, out_ref, logit_grad, left):
    sources, rows_kept, width = kept_ref.shape
    rows_per = width // 128
    packed = factor_ref[...]
    part = lax.broadcasted_iota(jnp.int32, packed.shape, 1) // 32

    def to_samples(index):
        spread = group_total(jnp.where(part == index, packed, 0.0))
        return jnp.broadcast_to(spread[:, None, :], (sources, rows_per, 128)).reshape(
            sources * rows_per, 128
        )

    taken = back_ref[0]
    taken_grad = 2.0 * to_samples(0) * taken + to_samples(1) * back_ref[3]
    behind, unused = scan_segment(taken_grad * taken, rows_per, False)
    grad = (taken_grad * back_ref[1] - behind - to_samples(2)) * back_ref[2]
    logit_grad[...] = grad.astype(bf16).astype(f32)

    def accumulate(source, total):
        for part_index in range(rows_per):
            lanes = pl.ds(part_index * 128, 128)
            row = logit_grad[pl.ds(source * rows_per + part_index, 1), :]
            hidden = kept_ref[source, pl.ds(32, 16), lanes].astype(f32)
            wide = jnp.broadcast_to(row, (16, 128))
            left[pl.ds(0, 16), lanes] = jnp.where(hidden > 0, wide, 0.0).astype(bf16)
            left[pl.ds(16, 16), lanes] = wide.astype(bf16)
        return total + lax.dot_general(
            left[...], kept_ref[source], LANES_BOTH, preferred_element_type=f32
        )

    total = lax.fori_loop(0, sources, accumulate, jnp.zeros((32, rows_kept), f32))
    in_ref[...] = total[0:16, 0:32] * prop_out_ref[...]
    out_ref[...] = total[16:17, 32:48]


def vmem():
    return pl.BlockSpec(memory_space=pltpu.VMEM)


def on_device(
    feature_grid,
    fine_in,
    fine_mid,
    fine_out,
    prop_in,
    prop_out,
    sample_cells,
    sample_geometry,
    slot_ray,
    slot_rank,
    bucket_count,
):
    sources = lax.axis_size("dom")
    capacity = slot_ray.shape[3]
    width = sample_cells.shape[3]
    rows_all = sources * width // 128
    slots = sources * capacity
    cell_total = feature_grid.shape[2]
    params = pltpu.CompilerParams(vmem_limit_bytes=58 * 2**20)

    arrived = lax.all_to_all(sample_geometry, "dom", split_axis=3, concat_axis=3, tiled=True)
    kept, back, stats = pl.pallas_call(
        owner_kernel,
        out_shape=(
            jax.ShapeDtypeStruct((sources, 48, width), bf16),
            jax.ShapeDtypeStruct((4, rows_all, 128), f32),
            jax.ShapeDtypeStruct((sources, 256), f32),
        ),
        in_specs=[pl.BlockSpec(memory_space=pltpu.SMEM)] + [vmem()] * 7,
        out_specs=(vmem(), vmem(), vmem()),
        scratch_shapes=[
            pltpu.VMEM((cell_total, 128), f32),
            pltpu.VMEM((TILE, 128), f32),
            pltpu.VMEM((TILE, 128), f32),
            pltpu.VMEM((TILE, 128), f32),
            pltpu.VMEM((TILE, 128), f32),
            pltpu.VMEM((4, sources, width), f32),
            pltpu.VMEM((rows_all, 128), f32),
            pltpu.VMEM((rows_all, 128), f32),
            pltpu.VMEM((rows_all, 128), f32),
        ],
        compiler_params=params,
        name="owner_forward",
    )(
        sample_cells.reshape(sources, width),
        arrived.reshape(4, sources, width),
        feature_grid[0],
        fine_in[0],
        fine_mid[0],
        fine_out,
        prop_in[0],
        prop_out,
    )
    returned = lax.all_to_all(stats, "dom", split_axis=0, concat_axis=0, tiled=True)
    by_slot = (
        returned.reshape(sources, 8, capacity).transpose(1, 0, 2).reshape(8, slots)
    )
    live = (
        (jnp.arange(capacity)[None, :] < bucket_count[0, 0][:, None]).astype(f32).reshape(1, slots)
    )
    factors, ray_loss = pl.pallas_call(
        ray_kernel,
        out_shape=(
            jax.ShapeDtypeStruct((4, slots), f32),
            jax.ShapeDtypeStruct((1, RAY_DEV), f32),
        ),
        in_specs=[vmem()] * 6,
        out_specs=(vmem(), vmem()),
        scratch_shapes=[pltpu.VMEM((slots, slots), bf16)],
        compiler_params=params,
        name="ray_side",
    )(
        by_slot,
        slot_ray.reshape(1, slots),
        slot_rank.reshape(1, slots),
        live,
        slot_ray.reshape(slots, 1),
        slot_rank.reshape(slots, 1),
    )
    by_owner = factors.reshape(4, sources, capacity).transpose(1, 0, 2).reshape(sources, 4 * capacity)
    owner_factors = lax.all_to_all(by_owner, "dom", split_axis=0, concat_axis=0, tiled=True)
    in_grad, out_grad = pl.pallas_call(
        backward_kernel,
        out_shape=(
            jax.ShapeDtypeStruct((16, 32), f32),
            jax.ShapeDtypeStruct((1, 16), f32),
        ),
        in_specs=[vmem()] * 4,
        out_specs=(vmem(), vmem()),
        scratch_shapes=[pltpu.VMEM((rows_all, 128), f32), pltpu.VMEM((32, width), bf16)],
        compiler_params=params,
        name="owner_backward",
    )(owner_factors, back, kept, prop_out[0].astype(f32)[:, None])
    in_sum, out_sum = lax.psum((in_grad, out_grad), "rep")
    return (ray_loss.reshape(1, 1, -1), in_sum[None], out_sum)


def solution(mesh):
    return jax.shard_map(
        on_device,
        mesh=mesh,
        in_specs=(
            P("dom", None, None),
            P("dom", None, None),
            P("dom", None, None, None),
            P("dom", None),
            P("dom", None, None),
            P("dom", None),
            P("dom", "rep", None, None),
            P(None, "dom", "rep", None, None),
            P("dom", "rep", None, None),
            P("dom", "rep", None, None),
            P("dom", "rep", None),
        ),
        out_specs=(P("dom", "rep", None), P("dom", None, None), P("dom", None)),
        check_vma=False,
    )
```

time: 651 us -> 341 us (0.52)
  local copies, waits for them, and re-layouts: 493 us -> 15.2 us
  Pallas kernels: 0 us -> 275 us
  matrix products: 60.8 us -> 0 us
  other arithmetic: 40.3 us -> 0.81 us
    gather x16 -> x0, local copies, waits for them, and re-layouts: 361 us -> none  [interpolate(): rows = jnp.take(table, cell_index, axis=0)]
    pallas_call x0 -> x3, Pallas kernels: none -> 275 us  [the longest x1 261 us: on_device(): pl.pallas_call(owner_kernel, out_shape=(jax.ShapeDtypeStruct((sources, 48...]
    concatenate x1 -> x0, local copies, waits for them, and re-layouts: 63.3 us -> none  [corner_table(): return jnp.concatenate(pieces, axis=1)]
    dot_general x69 -> x0, matrix products: 60.8 us -> none  [the longest x8 14.1 us: fine_density(): jnp.dot(fine_out, hidden_units, preferred_element_type=jnp.float32)]
    slice x10 -> x0, local copies, waits for them, and re-layouts: 48.9 us -> none  [the longest x1 47 us: corner_table(): pieces.append(padded[start:start + cell_total])]
    select_n x32 -> x0, other arithmetic: 21.8 us -> none  [the longest x16 21.4 us: interpolate(): rows = jnp.take(table, cell_index, axis=0)]
    dynamic_update_slice x8 -> x0, other arithmetic: 13.2 us -> none  [on_device(): lax.map(forward_group, (cell_groups, geometry_groups))]
    all_to_all x1, waiting for transfers between devices: 0.01 us -> 10.4 us  [on_device(): lax.all_to_all(sample_geometry, 'dom', split_axis=3, concat_axis=3, tiled...]
  transfers between devices with their start and end apart: 3 -> 3, of which waited for: 2 -> 3; matrix products, arithmetic and copies ran while one was open for 19% -> 2% of each run, Pallas kernels for 0% -> 0%
where the time goes in v1:
time: 341 us
  Pallas kernels  275 us (81%)
  waiting for transfers between devices  18.3 us (5%)
  starting transfers between devices  17.4 us (5%)
  local copies, waits for them, and re-layouts  15.2 us (4%)
  blocking collectives  12.7 us (4%)
    pallas_call x1, Pallas kernels, on_device(): pl.pallas_call(owner_kernel, out_shape=(jax.ShapeDtypeStruct((sources, 48...  261 us
    psum x1, blocking collectives, on_device(): in_sum, out_sum = lax.psum((in_grad, out_grad), 'rep')  12.7 us
    pallas_call x1, Pallas kernels, on_device(): pl.pallas_call(backward_kernel, out_shape=(jax.ShapeDtypeStruct((16, 32),...  10.7 us
    all_to_all x1, waiting for transfers between devices, on_device(): lax.all_to_all(sample_geometry, 'dom', split_axis=3, concat_axis=3, tiled...  10.4 us
    all_to_all x1, starting transfers between devices, on_device(): lax.all_to_all(sample_geometry, 'dom', split_axis=3, concat_axis=3, tiled...  7.41 us
  transfers between devices with their start and end apart: 3, of which 3 were waited for; matrix products, arithmetic and copies ran while one was open for 2% of the time, Pallas kernels for 0%

profile of v1, /device:TPU:0, one launch (start us, length us, event | category | flops | bytes accessed | tf_op | source)
XLA Modules:
  0.0 340.5 jit_solution(850149238773779069)
XLA Ops:
  0.7 2.3 copy.26
  2.9 7.4 %all-to-all-start = ((bf16[4,1,1,32,2048]{4,0,2,1,3:T(4,128)(2,1)}), bf16[4,1,1,32,2048]{4,0,2,1,3:T(4,128)(2,1)S(1)}, u32[]{:S(2)}, u32[]{:S(2)}) async-start(bf16[4,1,1,32,2048]{4,0,2,1,3:T(4,128)(2,1)} %copy.26), calls=%async_computation | async-start | bytes 1048576 | tf_op jit(solution)/shard_map/all_to_all | solution.py:293
  10.3 1.4 copy.28
  11.7 10.4 %all-to-all-done = bf16[4,1,1,32,2048]{4,0,2,1,3:T(4,128)(2,1)S(1)} async-done(((bf16[4,1,1,32,2048]{4,0,2,1,3:T(4,128)(2,1)}), bf16[4,1,1,32,2048]{4,0,2,1,3:T(4,128)(2,1)S(1)}, u32[]{:S(2)}, u32[]{:S(2)}) %all-to-all-start) | async-done | bytes 524320 | tf_op jit(solution)/shard_map/all_to_all | solution.py:293
  22.1 1.1 copy.37
  23.2 261.3 %owner_forward.1 = (bf16[32,48,2048]{2,1,0:T(8,128)(2,1)}, f32[4,512,128]{2,1,0:T(8,128)}, f32[32,256]{1,0:T(8,128)}) custom-call(s32[32,2048]{1,0:T(8,128)} %bitcast.32, bf16[4,32,2048]{2,1,0:T(8,128)(2,1)} %bitcast.29, bf16[32,32768]{1,0:T(8,128)(2,1)} %bitcast.28, bf16[64,32]{1,0:T(8,128)(2,1)} %bitcast.34, bf16[2,64,64]{2,1,0:T(8,128)(2,1)} %bitcast.35, ...), custom_call_target="tpu_custom_call" | custom-call | tf_op jit(solution)/shard_map/owner_forward/pallas_call | solution.py:294
  284.5 1.4 copy.29
  285.9 3.8 %all-to-all-start.1 = ((f32[32,1,256]{2,1,0:T(1,128)}), f32[32,1,256]{2,1,0:T(1,128)S(1)}, u32[]{:S(2)}, u32[]{:S(2)}) async-start(f32[32,1,256]{2,1,0:T(1,128)} %copy.29), calls=%async_computation.1 | async-start | bytes 65536 | tf_op jit(solution)/shard_map/all_to_all | solution.py:326
  289.7 0.7 fusion
  290.4 2.0 reshape.96.ray_col_ref
  292.5 0.7 reshape.88.ray_row_ref
  293.1 1.4 reshape.97.rank_col_ref
  294.5 0.7 reshape.89.rank_row_ref
  295.2 0.7 reshape.94.live_ref
  295.9 1.2 all-to-all-done.1
  297.3 0.7 reshape.87.stats_ref
  298.0 3.5 %ray_side.1 = (f32[4,1024]{1,0:T(4,128)}, f32[1,256]{1,0:T(1,128)}) custom-call(f32[8,1024]{1,0:T(8,128)} %reshape.87.stats_ref, s32[1,1024]{1,0:T(1,128)} %reshape.88.ray_row_ref, s32[1,1024]{1,0:T(1,128)} %reshape.89.rank_row_ref, f32[1,1024]{1,0:T(1,128)} %reshape.94.live_ref, s32[1024,1]{1,0:T(8,128)} %reshape.96.ray_col_ref, s32[1024,1]{1,0:T(8,128)} %reshape.97.rank_col_ref), custom_call_target="tpu_custom_call" | custom-call | tf_op jit(solution)/shard_map/ray_side/pallas_call | solution.py:333
  301.5 0.8 reshape.93
  302.3 0.7 all_to_all.19
  303.0 6.2 %all-to-all-start.2 = ((f32[32,1,128]{2,1,0:T(1,128)}), f32[32,1,128]{2,1,0:T(1,128)S(1)}, u32[]{:S(2)}, u32[]{:S(2)}) async-start(f32[32,1,128]{2,1,0:T(1,128)} %all_to_all.19), calls=%async_computation.2 | async-start | bytes 32768 | tf_op jit(solution)/shard_map/all_to_all | solution.py:353
  309.2 0.7 copy.34.prop_out_ref
  309.9 6.7 %all-to-all-done.2 = f32[32,1,128]{2,1,0:T(1,128)S(1)} async-done(((f32[32,1,128]{2,1,0:T(1,128)}), f32[32,1,128]{2,1,0:T(1,128)S(1)}, u32[]{:S(2)}, u32[]{:S(2)}) %all-to-all-start.2) | async-done | bytes 16416 | tf_op jit(solution)/shard_map/all_to_all | solution.py:353
  317.2 10.7 %owner_backward.1 = (f32[16,32]{1,0:T(8,128)}, f32[1,16]{1,0:T(1,128)}) custom-call(f32[32,128]{1,0:T(8,128)} %bitcast.33, f32[4,512,128]{2,1,0:T(8,128)} %get-tuple-element.13.back_ref, bf16[32,48,2048]{2,1,0:T(8,128)(2,1)} %get-tuple-element.14.kept_ref, f32[16,1]{1,0:T(8,128)} %copy.34.prop_out_ref), custom_call_target="tpu_custom_call" | custom-call | tf_op jit(solution)/shard_map/owner_backward/pallas_call | solution.py:354
  327.8 12.7 %all-reduce = (f32[1,16,32]{2,1,0:T(8,128)}, f32[1,16]{1,0:T(1,128)}) all-reduce(f32[1,16,32]{2,1,0:T(8,128)} %bitcast.37, f32[1,16]{1,0:T(1,128)} %get-tuple-element.16), channel_id=1, replica_groups=mesh['dom'=32,'rep'=4] {'rep'}, use_global_device_ids=true, to_apply=%region_0.0 | all-reduce | flops 528 | bytes 4224 | tf_op jit(solution)/shard_map/psum | solution.py:366
  (13 shorter events, 0.8 us)
Async XLA Ops:
  0.6 308.6 %copy-start.3 = (bf16[1,16]{1,0:T(2,128)(2,1)S(1)}, bf16[1,16]{1,0:T(2,128)(2,1)}, u32[]{:S(2)}) copy-start(bf16[1,16]{1,0:T(2,128)(2,1)} %prop_out_ref.1) | copy-start | bytes 100
  0.6 291.8 %copy-start.1 = (s32[1,1,32,32]{3,2,1,0:T(8,128)S(1)}, s32[1,1,32,32]{3,2,1,0:T(8,128)}, u32[]{:S(2)}) copy-start(s32[1,1,32,32]{3,2,1,0:T(8,128)} %param.19) | copy-start | bytes 12292
  0.7 292.5 %copy-start.2 = (s32[1,1,32,32]{3,2,1,0:T(8,128)S(1)}, s32[1,1,32,32]{3,2,1,0:T(8,128)}, u32[]{:S(2)}) copy-start(s32[1,1,32,32]{3,2,1,0:T(8,128)} %param.20) | copy-start | bytes 12292
  2.9 19.2 %all-to-all-start = ((bf16[4,1,1,32,2048]{4,0,2,1,3:T(4,128)(2,1)}), bf16[4,1,1,32,2048]{4,0,2,1,3:T(4,128)(2,1)S(1)}, u32[]{:S(2)}, u32[]{:S(2)}) async-start(bf16[4,1,1,32,2048]{4,0,2,1,3:T(4,128)(2,1)} %copy.26), calls=%async_computation | async-start | bytes 1048576 | tf_op jit(solution)/shard_map/all_to_all | solution.py:293
  285.9 11.2 %all-to-all-start.1 = ((f32[32,1,256]{2,1,0:T(1,128)}), f32[32,1,256]{2,1,0:T(1,128)S(1)}, u32[]{:S(2)}, u32[]{:S(2)}) async-start(f32[32,1,256]{2,1,0:T(1,128)} %copy.29), calls=%async_computation.1 | async-start | bytes 65536 | tf_op jit(solution)/shard_map/all_to_all | solution.py:326
  303.0 13.5 %all-to-all-start.2 = ((f32[32,1,128]{2,1,0:T(1,128)}), f32[32,1,128]{2,1,0:T(1,128)S(1)}, u32[]{:S(2)}, u32[]{:S(2)}) async-start(f32[32,1,128]{2,1,0:T(1,128)} %all_to_all.19), calls=%async_computation.2 | async-start | bytes 32768 | tf_op jit(solution)/shard_map/all_to_all | solution.py:353
  316.6 0.6 copy-start

commit v2 on v1

--- a/solution.py
+++ b/solution.py
@@ -9,7 +9,8 @@
 
 GR = 32
 RAY_DEV = 256
-TILE = 512
+TILE = 1024
+PART = 512
 
 distill_weight = 50.0
 f32 = jnp.float32
@@ -53,9 +54,9 @@
 def owner_kernel(
     cells_ref, geom_ref, grid_ref, fine_in_ref, fine_mid_ref, fine_out_ref, prop_in_ref, prop_out_ref,
     kept_ref, back_ref, stats_ref,
-    table, even0, even1, odd0, odd1, geo, fine_logit, prop_logit, spacing,
+    table, even, odd, geo, fine_logit, prop_logit, spacing, even_cells, odd_cells, sems,
 ):
-    sources, width = cells_ref.shape
+    sources, width = geom_ref.shape[1:]
     tiles_per = width // TILE
     tile_total = sources * tiles_per
     cell_blocks = grid_ref.shape[1] // 128
@@ -64,7 +65,7 @@
     geo[...] = geom_ref[...].astype(f32)
     lane = lax.broadcasted_iota(jnp.int32, (GR, 128), 1)
 
-    def build(block, carry):
+    def build(second, block, carry):
         here = grid_ref[:, pl.ds(pl.multiple_of(block * 128, 128), 128)].astype(f32)
         after = jnp.minimum(block + 1, cell_blocks - 1)
         there = grid_ref[:, pl.ds(pl.multiple_of(after * 128, 128), 128)].astype(f32)
@@ -77,12 +78,16 @@
                     pltpu.roll(there, 128 - shift, 1),
                 )
             )
-        table[pl.ds(pl.multiple_of(block * 128, 128), 128), :] = jnp.transpose(
-            jnp.concatenate(pieces, axis=0)
-        )
+        turned = jnp.transpose(jnp.concatenate(pieces, axis=0))
+        table[pl.ds(pl.multiple_of(block * 256, 256), 128, stride=2), :] = turned
+        if second:
+            earlier = pl.multiple_of((block - GR * GR // 128) * 256, 256)
+            table[pl.ds(earlier + 1, 128, stride=2), :] = turned
         return carry
 
-    lax.fori_loop(0, cell_blocks, build, 0, unroll=2)
+    slab = GR * GR // 128
+    lax.fori_loop(0, slab, functools.partial(build, False), 0)
+    lax.fori_loop(slab, cell_blocks, functools.partial(build, True), 0, unroll=2)
 
     first = jnp.concatenate([fine_in_ref[...], prop_in_ref[...]], axis=0)
     hidden = fine_in_ref.shape[0]
@@ -91,58 +96,99 @@
         == lax.broadcasted_iota(jnp.int32, (256, 256), 1)
     ).astype(f32).astype(bf16)
 
-    def gather(tile, low, high):
+    def fetch(tile, indices, sem):
+        start = pl.multiple_of(jnp.minimum(tile, tile_total - 1) * TILE, TILE)
+        return pltpu.make_async_copy(cells_ref.at[pl.ds(start, TILE)], indices, sem)
+
+    def gather(indices, low, start=0, stop=TILE):
+        for j in range(start, stop):
+            cell = pl.multiple_of(indices[j], 2)
+            low[pl.ds(2 * j, 2), :] = table[pl.ds(cell, 2), :]
+
+    def evaluate(tile, low, part):
         source = tile // tiles_per
-        base = (tile % tiles_per) * TILE
-        for j in range(TILE):
-            cell = cells_ref[source, base + j]
-            low[pl.ds(j, 1), :] = table[pl.ds(cell, 1), :]
-            high[pl.ds(j, 1), :] = table[pl.ds(cell + GR * GR, 1), :]
-
-    def evaluate(tile, low, high):
-        source = tile // tiles_per
-        lanes = pl.ds(pl.multiple_of((tile % tiles_per) * TILE, TILE), TILE)
-        rows = jnp.concatenate([low[...], high[...]], axis=1).astype(bf16)
-        turned = lax.dot_general(eye, rows, LANES_BOTH, preferred_element_type=f32)
-        offsets = [geo[axis, pl.ds(source, 1), lanes] for axis in range(3)]
-        factors = [[1.0 - value, value] for value in offsets]
-        summed = jnp.zeros((32, TILE), f32)
-        for corner in range(8):
-            factor = (
-                factors[0][corner // 4] * factors[1][corner // 2 % 2] * factors[2][corner % 2]
-            )
-            summed = summed + turned[corner * 32 : (corner + 1) * 32] * factor
-        features = summed.astype(bf16)
-        both = jnp.maximum(jnp.dot(first, features, preferred_element_type=f32), 0.0).astype(bf16)
-        prop_hidden = both[hidden:]
-        fine_hidden = both[:hidden]
-        kept_ref[source, pl.ds(0, 32), lanes] = features
-        kept_ref[source, pl.ds(32, 16), lanes] = prop_hidden
-        for layer in range(fine_mid_ref.shape[0]):
-            fine_hidden = jnp.maximum(
-                jnp.dot(fine_mid_ref[layer], fine_hidden, preferred_element_type=f32), 0.0
+        first_lane = (tile % tiles_per) * TILE
+        if True:
+            lanes = pl.ds(pl.multiple_of(first_lane + part * PART, PART), PART)
+            start = 2 * part * PART
+            rows = jnp.concatenate(
+                [
+                    low[pl.ds(start, PART, stride=2), :],
+                    low[pl.ds(start + 1, PART, stride=2), :],
+                ],
+                axis=1,
             ).astype(bf16)
-        fine = jnp.dot(fine_out_ref[...], fine_hidden, preferred_element_type=f32)
-        prop = jnp.dot(prop_out_ref[...], prop_hidden, preferred_element_type=f32)
-        step = geo[3, pl.ds(source, 1), lanes]
-        for part in range(TILE // 128):
-            row = pl.ds(tile * (TILE // 128) + part, 1)
-            cut = slice(part * 128, (part + 1) * 128)
-            fine_logit[row, :] = fine[:, cut]
-            prop_logit[row, :] = prop[:, cut]
-            spacing[row, :] = step[:, cut]
-
-    gather(0, even0, even1)
-
-    def pair(index, carry):
-        tile = index * 2
-        gather(tile + 1, odd0, odd1)
-        evaluate(tile, even0, even1)
-        gather(jnp.minimum(tile + 2, tile_total - 1), even0, even1)
-        evaluate(tile + 1, odd0, odd1)
+            turned = lax.dot_general(eye, rows, LANES_BOTH, preferred_element_type=f32)
+            yield
+            offsets = [geo[axis, pl.ds(source, 1), lanes] for axis in range(3)]
+            factors = [[1.0 - value, value] for value in offsets]
+            summed = jnp.zeros((32, PART), f32)
+            for corner in range(8):
+                factor = (
+                    factors[0][corner // 4]
+                    * factors[1][corner // 2 % 2]
+                    * factors[2][corner % 2]
+                )
+                summed = summed + turned[corner * 32 : (corner + 1) * 32] * factor
+            features = summed.astype(bf16)
+            kept_ref[source, pl.ds(0, 32), lanes] = features
+            yield
+            both = jnp.maximum(
+                jnp.dot(first, features, preferred_element_type=f32), 0.0
+            ).astype(bf16)
+            prop_hidden = both[hidden:]
+            fine_hidden = both[:hidden]
+            kept_ref[source, pl.ds(32, 16), lanes] = prop_hidden
+            yield
+            for layer in range(fine_mid_ref.shape[0]):
+                fine_hidden = jnp.maximum(
+                    jnp.dot(fine_mid_ref[layer], fine_hidden, preferred_element_type=f32), 0.0
+                ).astype(bf16)
+                yield
+            fine = jnp.dot(fine_out_ref[...], fine_hidden, preferred_element_type=f32)
+            prop = jnp.dot(prop_out_ref[...], prop_hidden, preferred_element_type=f32)
+            gap = geo[3, pl.ds(source, 1), lanes]
+            for piece in range(PART // 128):
+                row = pl.ds(tile * (TILE // 128) + (part * PART) // 128 + piece, 1)
+                cut = slice(piece * 128, (piece + 1) * 128)
+                fine_logit[row, :] = fine[:, cut]
+                prop_logit[row, :] = prop[:, cut]
+                spacing[row, :] = gap[:, cut]
+            yield
+
+    def weave(indices, into, tile, out_of):
+        parts = TILE // PART
+        stages = 4 + fine_mid_ref.shape[0]
+        slots = stages + parts - 1
+        running = [evaluate(tile, out_of, part) for part in range(parts)]
+        for slot in range(slots):
+            for part in range(parts):
+                if 0 <= slot - part < stages:
+                    next(running[part])
+            gather(indices, into, slot * TILE // slots, (slot + 1) * TILE // slots)
+
+    fetch(0, even_cells, sems.at[0]).start()
+    fetch(1, odd_cells, sems.at[1]).start()
+    fetch(0, even_cells, sems.at[0]).wait()
+    gather(even_cells, even)
+
+    def step(tile, carry):
+        @pl.when(tile % 2 == 0)
+        def _():
+            fetch(tile + 2, even_cells, sems.at[0]).start()
+            fetch(tile + 1, odd_cells, sems.at[1]).wait()
+            weave(odd_cells, odd, tile, even)
+
+        @pl.when(tile % 2 == 1)
+        def _():
+            fetch(tile + 2, odd_cells, sems.at[1]).start()
+            fetch(tile + 1, even_cells, sems.at[0]).wait()
+            weave(even_cells, even, tile, odd)
+
         return carry
 
-    lax.fori_loop(0, tile_total // 2, pair, 0)
+    lax.fori_loop(0, tile_total, step, 0)
+    fetch(tile_total, odd_cells, sems.at[1]).wait()
 
     gap = spacing[...]
     prop_raw = prop_logit[...]
@@ -298,23 +344,24 @@
             jax.ShapeDtypeStruct((4, rows_all, 128), f32),
             jax.ShapeDtypeStruct((sources, 256), f32),
         ),
-        in_specs=[pl.BlockSpec(memory_space=pltpu.SMEM)] + [vmem()] * 7,
+        in_specs=[pl.BlockSpec(memory_space=pl.ANY)] + [vmem()] * 7,
         out_specs=(vmem(), vmem(), vmem()),
         scratch_shapes=[
-            pltpu.VMEM((cell_total, 128), f32),
-            pltpu.VMEM((TILE, 128), f32),
-            pltpu.VMEM((TILE, 128), f32),
-            pltpu.VMEM((TILE, 128), f32),
-            pltpu.VMEM((TILE, 128), f32),
+            pltpu.VMEM((2 * cell_total, 128), f32),
+            pltpu.VMEM((2 * TILE, 128), f32),
+            pltpu.VMEM((2 * TILE, 128), f32),
             pltpu.VMEM((4, sources, width), f32),
             pltpu.VMEM((rows_all, 128), f32),
             pltpu.VMEM((rows_all, 128), f32),
             pltpu.VMEM((rows_all, 128), f32),
+            pltpu.SMEM((TILE,), jnp.int32),
+            pltpu.SMEM((TILE,), jnp.int32),
+            pltpu.SemaphoreType.DMA((2,)),
         ],
         compiler_params=params,
         name="owner_forward",
     )(
-        sample_cells.reshape(sources, width),
+        (sample_cells * 2).reshape(sources * width),
         arrived.reshape(4, sources, width),
         feature_grid[0],
         fine_in[0],

time: 341 us -> 174 us (0.51)
  Pallas kernels: 275 us -> 110 us
    pallas_call x1, Pallas kernels: 261 us -> 95.7 us  [on_device(): pl.pallas_call(owner_kernel, out_shape=(jax.ShapeDtypeStruct((sources, 48...]
  transfers between devices with their start and end apart: 3 -> 3, of which waited for: 3 -> 3; matrix products, arithmetic and copies ran while one was open for 2% -> 5% of each run, Pallas kernels for 0% -> 0%
where the time goes in v2:
time: 174 us
  Pallas kernels  110 us (63%)
  waiting for transfers between devices  17.9 us (10%)
  starting transfers between devices  16 us (9%)
  local copies, waits for them, and re-layouts  15.3 us (9%)
  blocking collectives  12.7 us (7%)
    pallas_call x1, Pallas kernels, on_device(): pl.pallas_call(owner_kernel, out_shape=(jax.ShapeDtypeStruct((sources, 48...  95.7 us
    psum x1, blocking collectives, on_device(): in_sum, out_sum = lax.psum((in_grad, out_grad), 'rep')  12.7 us
    pallas_call x1, Pallas kernels, on_device(): pl.pallas_call(backward_kernel, out_shape=(jax.ShapeDtypeStruct((16, 32),...  10.7 us
    all_to_all x1, waiting for transfers between devices, on_device(): lax.all_to_all(sample_geometry, 'dom', split_axis=3, concat_axis=3, tiled...  8.65 us
    all_to_all x1, starting transfers between devices, on_device(): lax.all_to_all(sample_geometry, 'dom', split_axis=3, concat_axis=3, tiled...  7.4 us
    all_to_all x1, waiting for transfers between devices, on_device(): lax.all_to_all(by_owner, 'dom', split_axis=0, concat_axis=0, tiled=True)  6.65 us
    unnamed x13, local copies, waits for them, and re-layouts  5.03 us
    all_to_all x1, starting transfers between devices, on_device(): lax.all_to_all(by_owner, 'dom', split_axis=0, concat_axis=0, tiled=True)  4.77 us
  transfers between devices with their start and end apart: 3, of which 3 were waited for; matrix products, arithmetic and copies ran while one was open for 5% of the time, Pallas kernels for 0%

profile of v2, /device:TPU:0, one launch (start us, length us, event | category | flops | bytes accessed | tf_op | source)
XLA Modules:
  0.0 173.6 jit_solution(12183660859844215347)
XLA Ops:
  0.7 2.3 %copy.26 = bf16[4,1,1,32,2048]{4,0,2,1,3:T(4,128)(2,1)} copy(bf16[4,1,1,32,2048]{4,3,2,1,0:T(8,128)(2,1)} %param.18) | data formatting | bytes 1048576 | tf_op args[7]
  2.9 7.4 %all-to-all-start = ((bf16[4,1,1,32,2048]{4,0,2,1,3:T(4,128)(2,1)}), bf16[4,1,1,32,2048]{4,0,2,1,3:T(4,128)(2,1)S(1)}, u32[]{:S(2)}, u32[]{:S(2)}) async-start(bf16[4,1,1,32,2048]{4,0,2,1,3:T(4,128)(2,1)} %copy.26), calls=%async_computation | async-start | bytes 1048576 | tf_op jit(solution)/shard_map/all_to_all | solution.py:339
  10.4 1.0 multiply_bitcast_fusion
  11.3 0.7 copy.35
  12.1 1.4 copy.28
  13.5 8.7 %all-to-all-done = bf16[4,1,1,32,2048]{4,0,2,1,3:T(4,128)(2,1)S(1)} async-done(((bf16[4,1,1,32,2048]{4,0,2,1,3:T(4,128)(2,1)}), bf16[4,1,1,32,2048]{4,0,2,1,3:T(4,128)(2,1)S(1)}, u32[]{:S(2)}, u32[]{:S(2)}) %all-to-all-start) | async-done | bytes 524320 | tf_op jit(solution)/shard_map/all_to_all | solution.py:339
  22.1 1.1 copy.38
  23.2 95.7 %owner_forward.1 = (bf16[32,48,2048]{2,1,0:T(8,128)(2,1)}, f32[4,512,128]{2,1,0:T(8,128)}, f32[32,256]{1,0:T(8,128)}) custom-call(s32[65536]{0:T(1024)} %bitcast.32, bf16[4,32,2048]{2,1,0:T(8,128)(2,1)} %bitcast.31, bf16[32,32768]{1,0:T(8,128)(2,1)} %bitcast.30, bf16[64,32]{1,0:T(8,128)(2,1)} %bitcast.36, bf16[2,64,64]{2,1,0:T(8,128)(2,1)} %bitcast.37, ...), custom_call_target="tpu_custom_call" | custom-call | tf_op jit(solution)/shard_map/owner_forward/pallas_call | solution.py:340
  118.9 1.4 copy.29
  120.3 3.8 %all-to-all-start.1 = ((f32[32,1,256]{2,1,0:T(1,128)}), f32[32,1,256]{2,1,0:T(1,128)S(1)}, u32[]{:S(2)}, u32[]{:S(2)}) async-start(f32[32,1,256]{2,1,0:T(1,128)} %copy.29), calls=%async_computation.1 | async-start | bytes 65536 | tf_op jit(solution)/shard_map/all_to_all | solution.py:373
  124.2 1.3 reshape.96.ray_col_ref
  125.6 0.7 reshape.88.ray_row_ref
  126.2 1.4 reshape.97.rank_col_ref
  127.6 0.7 reshape.89.rank_row_ref
  129.0 2.6 %all-to-all-done.1 = f32[32,1,256]{2,1,0:T(1,128)S(1)} async-done(((f32[32,1,256]{2,1,0:T(1,128)}), f32[32,1,256]{2,1,0:T(1,128)S(1)}, u32[]{:S(2)}, u32[]{:S(2)}) %all-to-all-start.1) | async-done | bytes 32800 | tf_op jit(solution)/shard_map/all_to_all | solution.py:373
  131.8 0.7 reshape.87.stats_ref
  132.5 3.5 %ray_side.1 = (f32[4,1024]{1,0:T(4,128)}, f32[1,256]{1,0:T(1,128)}) custom-call(f32[8,1024]{1,0:T(8,128)} %reshape.87.stats_ref, s32[1,1024]{1,0:T(1,128)} %reshape.88.ray_row_ref, s32[1,1024]{1,0:T(1,128)} %reshape.89.rank_row_ref, f32[1,1024]{1,0:T(1,128)} %reshape.94.live_ref, s32[1024,1]{1,0:T(8,128)} %reshape.96.ray_col_ref, s32[1024,1]{1,0:T(8,128)} %reshape.97.rank_col_ref), custom_call_target="tpu_custom_call" | custom-call | tf_op jit(solution)/shard_map/ray_side/pallas_call | solution.py:380
  135.9 0.8 reshape.93
  136.8 0.7 all_to_all.19
  137.5 4.8 %all-to-all-start.2 = ((f32[32,1,128]{2,1,0:T(1,128)}), f32[32,1,128]{2,1,0:T(1,128)S(1)}, u32[]{:S(2)}, u32[]{:S(2)}) async-start(f32[32,1,128]{2,1,0:T(1,128)} %all_to_all.19), calls=%async_computation.2 | async-start | bytes 32768 | tf_op jit(solution)/shard_map/all_to_all | solution.py:400
  142.3 0.7 copy.34.prop_out_ref
  143.0 6.7 %all-to-all-done.2 = f32[32,1,128]{2,1,0:T(1,128)S(1)} async-done(((f32[32,1,128]{2,1,0:T(1,128)}), f32[32,1,128]{2,1,0:T(1,128)S(1)}, u32[]{:S(2)}, u32[]{:S(2)}) %all-to-all-start.2) | async-done | bytes 16416 | tf_op jit(solution)/shard_map/all_to_all | solution.py:400
  150.3 10.7 %owner_backward.1 = (f32[16,32]{1,0:T(8,128)}, f32[1,16]{1,0:T(1,128)}) custom-call(f32[32,128]{1,0:T(8,128)} %bitcast.35, f32[4,512,128]{2,1,0:T(8,128)} %get-tuple-element.13.back_ref, bf16[32,48,2048]{2,1,0:T(8,128)(2,1)} %get-tuple-element.14.kept_ref, f32[16,1]{1,0:T(8,128)} %copy.34.prop_out_ref), custom_call_target="tpu_custom_call" | custom-call | tf_op jit(solution)/shard_map/owner_backward/pallas_call | solution.py:401
  160.9 12.7 %all-reduce = (f32[1,16,32]{2,1,0:T(8,128)}, f32[1,16]{1,0:T(1,128)}) all-reduce(f32[1,16,32]{2,1,0:T(8,128)} %bitcast.39, f32[1,16]{1,0:T(1,128)} %get-tuple-element.16), channel_id=1, replica_groups=mesh['dom'=32,'rep'=4] {'rep'}, use_global_device_ids=true, to_apply=%region_0.0 | all-reduce | flops 528 | bytes 4224 | tf_op jit(solution)/shard_map/psum | solution.py:413
  (17 shorter events, 1.6 us)
Async XLA Ops:
  0.6 141.7 %copy-start.4 = (bf16[1,16]{1,0:T(2,128)(2,1)S(1)}, bf16[1,16]{1,0:T(2,128)(2,1)}, u32[]{:S(2)}) copy-start(bf16[1,16]{1,0:T(2,128)(2,1)} %prop_out_ref.1) | copy-start | bytes 100
  0.6 123.5 %copy-start.3 = (s32[1,1,32]{2,1,0:T(1,128)S(1)}, s32[1,1,32]{2,1,0:T(1,128)}, u32[]{:S(2)}) copy-start(s32[1,1,32]{2,1,0:T(1,128)} %param.21) | copy-start | bytes 388
  0.7 123.6 %copy-start.1 = (s32[1,1,32,32]{3,2,1,0:T(8,128)S(1)}, s32[1,1,32,32]{3,2,1,0:T(8,128)}, u32[]{:S(2)}) copy-start(s32[1,1,32,32]{3,2,1,0:T(8,128)} %param.19) | copy-start | bytes 12292
  0.7 125.6 %copy-start.2 = (s32[1,1,32,32]{3,2,1,0:T(8,128)S(1)}, s32[1,1,32,32]{3,2,1,0:T(8,128)}, u32[]{:S(2)}) copy-start(s32[1,1,32,32]{3,2,1,0:T(8,128)} %param.20) | copy-start | bytes 12292
  2.9 19.2 %all-to-all-start = ((bf16[4,1,1,32,2048]{4,0,2,1,3:T(4,128)(2,1)}), bf16[4,1,1,32,2048]{4,0,2,1,3:T(4,128)(2,1)S(1)}, u32[]{:S(2)}, u32[]{:S(2)}) async-start(bf16[4,1,1,32,2048]{4,0,2,1,3:T(4,128)(2,1)} %copy.26), calls=%async_computation | async-start | bytes 1048576 | tf_op jit(solution)/shard_map/all_to_all | solution.py:339
  120.3 11.3 %all-to-all-start.1 = ((f32[32,1,256]{2,1,0:T(1,128)}), f32[32,1,256]{2,1,0:T(1,128)S(1)}, u32[]{:S(2)}, u32[]{:S(2)}) async-start(f32[32,1,256]{2,1,0:T(1,128)} %copy.29), calls=%async_computation.1 | async-start | bytes 65536 | tf_op jit(solution)/shard_map/all_to_all | solution.py:373
  137.5 12.1 %all-to-all-start.2 = ((f32[32,1,128]{2,1,0:T(1,128)}), f32[32,1,128]{2,1,0:T(1,128)S(1)}, u32[]{:S(2)}, u32[]{:S(2)}) async-start(f32[32,1,128]{2,1,0:T(1,128)} %all_to_all.19), calls=%async_computation.2 | async-start | bytes 32768 | tf_op jit(solution)/shard_map/all_to_all | solution.py:400
  149.6 0.6 copy-start

commit v3 on v2

--- a/solution.py
+++ b/solution.py
@@ -16,6 +16,7 @@
 f32 = jnp.float32
 bf16 = jnp.bfloat16
 LANES_BOTH = (((1,), (1,)), ((), ()))
+MESH = pl.DeviceIdType.MESH
 
 
 def softplus(x):
@@ -214,10 +215,10 @@
     log_prop = -per_segment(prop_total, True)
     log_fine = -per_segment(fine_total, True)
     part = lax.broadcasted_iota(jnp.int32, (sources, 128), 1) // 32
-    stats_ref[:, pl.ds(0, 128)] = jnp.where(
+    stats_ref[:, 0, :] = jnp.where(
         part == 0, sum_aa, jnp.where(part == 1, sum_ab, jnp.where(part == 2, sum_bb, log_prop))
     )
-    stats_ref[:, pl.ds(128, 128)] = log_fine
+    stats_ref[:, 1, :] = log_fine
 
 
 def split_three(value):
@@ -228,12 +229,133 @@
     return [high, middle, low]
 
 
-def ray_kernel(stats_ref, ray_row_ref, rank_row_ref, live_ref, ray_col_ref, rank_col_ref, factor_ref, loss_ref, ahead):
-    slots = stats_ref.shape[1]
-    key_row = ray_row_ref[...] * 64 + rank_row_ref[...]
-    rank_row = rank_row_ref[...]
-    live = live_ref[...]
-    sum_aa, sum_ab, sum_bb, log_prop, log_fine = (stats_ref[pl.ds(i, 1), :] for i in range(5))
+def finish_kernel(
+    stats_ref, ray_ref, rank_ref, count_ref, prop_out_ref, back_hbm, kept_hbm,
+    loss_ref, in_ref, out_ref,
+    stats_in, factors_out, factors_in, grads_in, flat, ahead, logit_grad, left, back_ref, kept_ref,
+    stats_send, stats_recv, factors_send, factors_recv, grads_send, grads_recv, local,
+):
+    sources, rows_kept, width = kept_ref.shape
+    rows_per = width // 128
+    slots = ahead.shape[0]
+    blocks = slots // 128
+    me, replica = lax.axis_index("dom"), lax.axis_index("rep")
+    replicas = lax.axis_size("rep")
+
+    load_kept = pltpu.make_async_copy(kept_hbm, kept_ref, local.at[0])
+    load_back = pltpu.make_async_copy(back_hbm, back_ref, local.at[1])
+    load_back.start()
+    load_kept.start()
+
+    barrier = pltpu.get_barrier_semaphore()
+
+    def greet(step, carry):
+        peer = lax.rem(me + step, sources)
+        pl.semaphore_signal(barrier, inc=1, device_id=(peer, replica), device_id_type=MESH)
+        return carry
+
+    lax.fori_loop(1, sources, greet, 0)
+    for step in range(1, replicas):
+        other = lax.rem(replica + step, replicas)
+        pl.semaphore_signal(barrier, inc=1, device_id=(me, other), device_id_type=MESH)
+    pl.semaphore_wait(barrier, sources + replicas - 2)
+
+    def exchange(source, target, send, recv):
+        def copy(step):
+            peer = lax.rem(me + step, sources)
+            return pltpu.make_async_remote_copy(
+                src_ref=source.at[peer],
+                dst_ref=target.at[me],
+                send_sem=send.at[step],
+                recv_sem=recv.at[step],
+                device_id=(peer, replica),
+                device_id_type=MESH,
+            )
+
+        def start(step, carry):
+            copy(step).start()
+            return carry
+
+        def finish(step, carry):
+            copy(step).wait()
+            return carry
+
+        lax.fori_loop(1, sources, start, 0)
+        return lambda: lax.fori_loop(1, sources, finish, 0)
+
+    wait_stats = exchange(stats_ref, stats_in, stats_send, stats_recv)
+    own_stats = pltpu.make_async_copy(stats_ref.at[me], stats_in.at[me], local.at[2])
+    own_stats.start()
+
+    part_row = lax.broadcasted_iota(jnp.int32, (sources, 128), 0)
+    group = lax.broadcasted_iota(jnp.int32, (sources, 128), 1) // 32
+    seat = part_row % 4
+    fold = jnp.where(
+        lax.broadcasted_iota(jnp.int32, (blocks, sources), 0)
+        == lax.broadcasted_iota(jnp.int32, (blocks, sources), 1) // 4,
+        1.0,
+        0.0,
+    )
+    unfold = jnp.where(
+        lax.broadcasted_iota(jnp.int32, (sources, blocks), 0) // 4
+        == lax.broadcasted_iota(jnp.int32, (sources, blocks), 1),
+        1.0,
+        0.0,
+    )
+
+    def exact(first, second):
+        return jnp.dot(first, second, precision=lax.Precision.HIGHEST, preferred_element_type=f32)
+
+    def dense(seated):
+        return exact(fold, jnp.where(group == seat, seated, 0.0))
+
+    def four(value):
+        return jnp.concatenate([value] * 4, axis=1)
+
+    def as_row(value):
+        return jnp.concatenate([value[b : b + 1] for b in range(blocks)], axis=1)
+
+    def as_dense(value):
+        return jnp.concatenate(
+            [value[:, b * 128 : (b + 1) * 128] for b in range(blocks)], axis=0
+        )
+
+    counts = jnp.broadcast_to(count_ref[...].astype(f32), (sources, sources))
+    diagonal = lax.broadcasted_iota(jnp.int32, (sources, sources), 0) == lax.broadcasted_iota(
+        jnp.int32, (sources, sources), 1
+    )
+    count_column = jnp.sum(jnp.where(diagonal, counts, 0.0), axis=1, keepdims=True)
+    slot_lane = (lax.broadcasted_iota(jnp.int32, (sources, 128), 1) % 32).astype(f32)
+    live = as_row(dense(jnp.where(slot_lane < count_column, 1.0, 0.0)))
+    rays = dense(four(ray_ref[...].astype(f32)))
+    ranks = dense(four(rank_ref[...].astype(f32)))
+    keys = rays * 64.0 + ranks
+    key_row, rank_row = as_row(keys), as_row(ranks)
+    key_column, ray_column = jnp.transpose(keys), jnp.transpose(rays)
+    for chunk in range(blocks):
+        gap = key_row - key_column[:, chunk : chunk + 1]
+        ahead[pl.ds(chunk * 128, 128), :] = jnp.where(
+            (gap > 0.5) & (gap < rank_row + 0.5), 1.0, 0.0
+        ).astype(bf16)
+
+    own_stats.wait()
+    wait_stats()
+
+    for index in range(sources):
+        flat[pl.ds(index, 1), :] = stats_in[index, pl.ds(0, 1), :]
+    packed = flat[...]
+    turned = [packed] + [pltpu.roll(packed, 32 * step, 1) for step in range(1, 4)]
+
+    def stat(index):
+        value = turned[(3 - index) % 4]
+        for place in range(3):
+            value = jnp.where(seat == place, turned[(place - index) % 4], value)
+        return as_row(dense(value))
+
+    sum_aa, sum_ab, sum_bb, log_prop = (stat(index) for index in range(4))
+    for index in range(sources):
+        flat[pl.ds(index, 1), :] = stats_in[index, pl.ds(1, 1), :]
+    log_fine = as_row(dense(flat[...]))
 
     def stacked(values):
         pieces = [piece.astype(f32) for value in values for piece in split_three(value)]
@@ -241,49 +363,58 @@
         return jnp.concatenate(pieces, axis=0).astype(bf16)
 
     logs = stacked([log_prop * live, log_fine * live])
-    reached = jnp.zeros((8, slots), f32)
-    for chunk in range(slots // 128):
-        rows = pl.ds(chunk * 128, 128)
-        gap = key_row - (ray_col_ref[rows, :] * 64 + rank_col_ref[rows, :])
-        mask = jnp.where((gap > 0) & (gap <= rank_row), 1.0, 0.0).astype(bf16)
-        ahead[rows, :] = mask
-        reached = reached + jnp.dot(
-            logs[:, chunk * 128 : (chunk + 1) * 128], mask, preferred_element_type=f32
-        )
+    reached = jnp.dot(logs, ahead[...], preferred_element_type=f32)
     entry_prop = jnp.exp(reached[0:1] + reached[1:2] + reached[2:3]) * live
     entry_fine = jnp.exp(reached[3:4] + reached[4:5] + reached[5:6]) * live
+    slot_grad = distill_weight * (entry_prop * sum_aa - entry_fine * sum_ab) * entry_prop
+    carried = lax.dot_general(
+        stacked([slot_grad]), ahead[...], LANES_BOTH, preferred_element_type=f32
+    )
+    outgoing = (
+        0.5 * distill_weight * entry_prop * entry_prop,
+        -distill_weight * entry_prop * entry_fine,
+        (carried[0:1] + carried[1:2] + carried[2:3]) * live,
+    )
+    message = jnp.zeros((sources, 128), f32)
+    for index, value in enumerate(outgoing):
+        spread = exact(unfold, as_dense(value))
+        for place in range(4):
+            shift = 32 * ((index - place) % 4)
+            moved = pltpu.roll(spread, shift, 1) if shift else spread
+            message = jnp.where((group == index) & (seat == place), moved, message)
+    for index in range(sources):
+        factors_out[index] = message[index : index + 1]
+
+    wait_factors = exchange(factors_out, factors_in, factors_send, factors_recv)
+    own_factors = pltpu.make_async_copy(factors_out.at[me], factors_in.at[me], local.at[3])
+    own_factors.start()
+
     seg_loss = (
         entry_prop * entry_prop * sum_aa
         - 2.0 * entry_prop * entry_fine * sum_ab
         + entry_fine * entry_fine * sum_bb
     )
-    slot_grad = distill_weight * (entry_prop * sum_aa - entry_fine * sum_ab) * entry_prop
-    carried = lax.dot_general(
-        stacked([slot_grad]), ahead[...], LANES_BOTH, preferred_element_type=f32
-    )
-    factor_ref[pl.ds(0, 1), :] = 0.5 * distill_weight * entry_prop * entry_prop
-    factor_ref[pl.ds(1, 1), :] = -distill_weight * entry_prop * entry_fine
-    factor_ref[pl.ds(2, 1), :] = (carried[0:1] + carried[1:2] + carried[2:3]) * live
-    factor_ref[pl.ds(3, 1), :] = jnp.zeros_like(live)
     losses = stacked([seg_loss])
     ray_loss = jnp.zeros((8, RAY_DEV), f32)
-    ray_ids = lax.broadcasted_iota(jnp.int32, (128, RAY_DEV), 1)
-    for chunk in range(slots // 128):
-        mask = jnp.where(ray_col_ref[pl.ds(chunk * 128, 128), :] == ray_ids, 1.0, 0.0).astype(bf16)
+    ray_ids = lax.broadcasted_iota(jnp.int32, (128, RAY_DEV), 1).astype(f32)
+    for chunk in range(blocks):
+        mask = jnp.where(ray_column[:, chunk : chunk + 1] == ray_ids, 1.0, 0.0).astype(bf16)
         ray_loss = ray_loss + jnp.dot(
             losses[:, chunk * 128 : (chunk + 1) * 128], mask, preferred_element_type=f32
         )
     loss_ref[...] = 0.5 * distill_weight * (ray_loss[0:1] + ray_loss[1:2] + ray_loss[2:3])
 
-
-def backward_kernel(factor_ref, back_ref, kept_ref, prop_out_ref, in_ref, out_ref, logit_grad, left):
-    sources, rows_kept, width = kept_ref.shape
-    rows_per = width // 128
-    packed = factor_ref[...]
-    part = lax.broadcasted_iota(jnp.int32, packed.shape, 1) // 32
+    load_back.wait()
+    load_kept.wait()
+    own_factors.wait()
+    wait_factors()
+
+    for index in range(sources):
+        flat[pl.ds(index, 1), :] = factors_in[index]
+    factors = flat[...]
 
     def to_samples(index):
-        spread = group_total(jnp.where(part == index, packed, 0.0))
+        spread = group_total(jnp.where(group == index, factors, 0.0))
         return jnp.broadcast_to(spread[:, None, :], (sources, rows_per, 128)).reshape(
             sources * rows_per, 128
         )
@@ -307,8 +438,28 @@
         )
 
     total = lax.fori_loop(0, sources, accumulate, jnp.zeros((32, rows_kept), f32))
-    in_ref[...] = total[0:16, 0:32] * prop_out_ref[...]
-    out_ref[...] = total[16:17, 32:48]
+    grads_in[replica] = jnp.concatenate([total, jnp.zeros((32, 128 - rows_kept), f32)], axis=1)
+
+    def share(step):
+        other = lax.rem(replica + step, replicas)
+        return pltpu.make_async_remote_copy(
+            src_ref=grads_in.at[replica],
+            dst_ref=grads_in.at[replica],
+            send_sem=grads_send.at[step],
+            recv_sem=grads_recv.at[step],
+            device_id=(me, other),
+            device_id_type=MESH,
+        )
+
+    for step in range(1, replicas):
+        share(step).start()
+    for step in range(1, replicas):
+        share(step).wait()
+    summed = grads_in[0]
+    for index in range(1, replicas):
+        summed = summed + grads_in[index]
+    in_ref[...] = summed[0:16, 0:32] * prop_out_ref[...]
+    out_ref[...] = summed[16:17, 32:48]
 
 
 def vmem():
@@ -342,7 +493,7 @@
         out_shape=(
             jax.ShapeDtypeStruct((sources, 48, width), bf16),
             jax.ShapeDtypeStruct((4, rows_all, 128), f32),
-            jax.ShapeDtypeStruct((sources, 256), f32),
+            jax.ShapeDtypeStruct((sources, 2, 128), f32),
         ),
         in_specs=[pl.BlockSpec(memory_space=pl.ANY)] + [vmem()] * 7,
         out_specs=(vmem(), vmem(), vmem()),
@@ -370,47 +521,47 @@
         prop_in[0],
         prop_out,
     )
-    returned = lax.all_to_all(stats, "dom", split_axis=0, concat_axis=0, tiled=True)
-    by_slot = (
-        returned.reshape(sources, 8, capacity).transpose(1, 0, 2).reshape(8, slots)
-    )
-    live = (
-        (jnp.arange(capacity)[None, :] < bucket_count[0, 0][:, None]).astype(f32).reshape(1, slots)
-    )
-    factors, ray_loss = pl.pallas_call(
-        ray_kernel,
+    ray_loss, in_sum, out_sum = pl.pallas_call(
+        finish_kernel,
         out_shape=(
-            jax.ShapeDtypeStruct((4, slots), f32),
             jax.ShapeDtypeStruct((1, RAY_DEV), f32),
-        ),
-        in_specs=[vmem()] * 6,
-        out_specs=(vmem(), vmem()),
-        scratch_shapes=[pltpu.VMEM((slots, slots), bf16)],
-        compiler_params=params,
-        name="ray_side",
-    )(
-        by_slot,
-        slot_ray.reshape(1, slots),
-        slot_rank.reshape(1, slots),
-        live,
-        slot_ray.reshape(slots, 1),
-        slot_rank.reshape(slots, 1),
-    )
-    by_owner = factors.reshape(4, sources, capacity).transpose(1, 0, 2).reshape(sources, 4 * capacity)
-    owner_factors = lax.all_to_all(by_owner, "dom", split_axis=0, concat_axis=0, tiled=True)
-    in_grad, out_grad = pl.pallas_call(
-        backward_kernel,
-        out_shape=(
             jax.ShapeDtypeStruct((16, 32), f32),
             jax.ShapeDtypeStruct((1, 16), f32),
         ),
-        in_specs=[vmem()] * 4,
-        out_specs=(vmem(), vmem()),
-        scratch_shapes=[pltpu.VMEM((rows_all, 128), f32), pltpu.VMEM((32, width), bf16)],
-        compiler_params=params,
-        name="owner_backward",
-    )(owner_factors, back, kept, prop_out[0].astype(f32)[:, None])
-    in_sum, out_sum = lax.psum((in_grad, out_grad), "rep")
+        in_specs=[vmem()] * 5 + [pl.BlockSpec(memory_space=pl.ANY)] * 2,
+        out_specs=(vmem(), vmem(), vmem()),
+        scratch_shapes=[
+            pltpu.VMEM((sources, 2, 128), f32),
+            pltpu.VMEM((sources, 1, 128), f32),
+            pltpu.VMEM((sources, 1, 128), f32),
+            pltpu.VMEM((lax.axis_size("rep"), 32, 128), f32),
+            pltpu.VMEM((sources, 128), f32),
+            pltpu.VMEM((slots, slots), bf16),
+            pltpu.VMEM((rows_all, 128), f32),
+            pltpu.VMEM((32, width), bf16),
+            pltpu.VMEM((4, rows_all, 128), f32),
+            pltpu.VMEM((sources, 48, width), bf16),
+            pltpu.SemaphoreType.DMA((sources,)),
+            pltpu.SemaphoreType.DMA((sources,)),
+            pltpu.SemaphoreType.DMA((sources,)),
+            pltpu.SemaphoreType.DMA((sources,)),
+            pltpu.SemaphoreType.DMA((lax.axis_size("rep"),)),
+            pltpu.SemaphoreType.DMA((lax.axis_size("rep"),)),
+            pltpu.SemaphoreType.DMA((4,)),
+        ],
+        compiler_params=pltpu.CompilerParams(
+            vmem_limit_bytes=58 * 2**20, collective_id=0, has_side_effects=True
+        ),
+        name="finish",
+    )(
+        stats,
+        slot_ray[0, 0],
+        slot_rank[0, 0],
+        bucket_count[0],
+        prop_out[0].astype(f32)[:, None],
+        back,
+        kept,
+    )
     return (ray_loss.reshape(1, 1, -1), in_sum[None], out_sum)
 
 

time: 174 us -> 152 us (0.87)
  Pallas kernels: 110 us -> 124 us
  blocking collectives: 12.7 us -> 0 us
  waiting for transfers between devices: 17.9 us -> 7.31 us
  starting transfers between devices: 16 us -> 7.4 us
  local copies, waits for them, and re-layouts: 15.3 us -> 9.73 us
    pallas_call x2 -> x1, Pallas kernels: 14.1 us -> 28.7 us  [on_device(): pl.pallas_call(finish_kernel, out_shape=(jax.ShapeDtypeStruct((1, RAY_DEV...]
    psum x1 -> x0, blocking collectives: 12.7 us -> none  [on_device(): in_sum, out_sum = lax.psum((in_grad, out_grad), 'rep')]
    all_to_all x2 -> x0, waiting for transfers between devices: 9.26 us -> none  [the longest x1 6.65 us: on_device(): lax.all_to_all(by_owner, 'dom', split_axis=0, concat_axis=0, tiled=True)]
    all_to_all x2 -> x0, starting transfers between devices: 8.61 us -> none  [the longest x1 4.77 us: on_device(): lax.all_to_all(by_owner, 'dom', split_axis=0, concat_axis=0, tiled=True)]
    reshape x8 -> x0, local copies, waits for them, and re-layouts: 5.67 us -> none  [the longest x1 1.38 us: on_device(): slot_rank.reshape(slots, 1)]
    unnamed x13 -> x6, local copies, waits for them, and re-layouts: 5.03 us -> 7.98 us
    all_to_all x2 -> x0, local copies, waits for them, and re-layouts: 2.1 us -> none  [the longest x1 1.39 us: on_device(): lax.all_to_all(stats, 'dom', split_axis=0, concat_axis=0, tiled=True)]
  transfers between devices with their start and end apart: 3 -> 1, of which waited for: 3 -> 1; matrix products, arithmetic and copies ran while one was open for 5% -> 3% of each run, Pallas kernels for 0% -> 0%
where the time goes in v3:
time: 152 us; the launch traced here: 151 us
  Pallas kernels  124 us (82%)
  local copies, waits for them, and re-layouts  9.73 us (6%)
  starting transfers between devices  7.4 us (5%)
  waiting for transfers between devices  7.31 us (5%)
  other arithmetic  1.63 us (1%)
    pallas_call x1, Pallas kernels, on_device(): pl.pallas_call(owner_kernel, out_shape=(jax.ShapeDtypeStruct((sources, 48...  95.7 us
    pallas_call x1, Pallas kernels, on_device(): pl.pallas_call(finish_kernel, out_shape=(jax.ShapeDtypeStruct((1, RAY_DEV...  28.7 us
    unnamed x6, local copies, waits for them, and re-layouts  7.98 us
    all_to_all x1, starting transfers between devices, on_device(): lax.all_to_all(sample_geometry, 'dom', split_axis=3, concat_axis=3, tiled...  7.4 us
    all_to_all x1, waiting for transfers between devices, on_device(): lax.all_to_all(sample_geometry, 'dom', split_axis=3, concat_axis=3, tiled...  7.31 us
  transfers between devices with their start and end apart: 1, of which 1 were waited for; matrix products, arithmetic and copies ran while one was open for 3% of the time, Pallas kernels for 0%

profile of v3, /device:TPU:0, one launch (start us, length us, event | category | flops | bytes accessed | tf_op | source)
XLA Modules:
  0.0 151.1 jit_solution(8602597368088318376)
XLA Ops:
  0.6 2.2 %copy.17 = bf16[4,1,1,32,2048]{4,0,2,1,3:T(4,128)(2,1)} copy(bf16[4,1,1,32,2048]{4,3,2,1,0:T(8,128)(2,1)} %param.18) | data formatting | bytes 1048576 | tf_op args[7]
  2.9 7.4 %all-to-all-start = ((bf16[4,1,1,32,2048]{4,0,2,1,3:T(4,128)(2,1)}), bf16[4,1,1,32,2048]{4,0,2,1,3:T(4,128)(2,1)S(1)}, u32[]{:S(2)}, u32[]{:S(2)}) async-start(bf16[4,1,1,32,2048]{4,0,2,1,3:T(4,128)(2,1)} %copy.17), calls=%async_computation | async-start | bytes 1048576 | tf_op jit(solution)/shard_map/all_to_all | solution.py:490
  10.3 1.0 multiply_bitcast_fusion
  11.3 0.8 copy.21
  12.0 1.4 copy.19
  13.4 0.7 bitcast_convert_fusion
  14.0 0.7 copy.20.prop_out_ref
  14.7 7.3 %all-to-all-done = bf16[4,1,1,32,2048]{4,0,2,1,3:T(4,128)(2,1)S(1)} async-done(((bf16[4,1,1,32,2048]{4,0,2,1,3:T(4,128)(2,1)}), bf16[4,1,1,32,2048]{4,0,2,1,3:T(4,128)(2,1)S(1)}, u32[]{:S(2)}, u32[]{:S(2)}) %all-to-all-start) | async-done | bytes 524320 | tf_op jit(solution)/shard_map/all_to_all | solution.py:490
  22.0 1.1 copy.23
  23.1 95.7 %owner_forward.1 = (bf16[32,48,2048]{2,1,0:T(8,128)(2,1)}, f32[4,512,128]{2,1,0:T(8,128)}, f32[32,2,128]{2,1,0:T(2,128)}) custom-call(s32[65536]{0:T(1024)} %bitcast.20, bf16[4,32,2048]{2,1,0:T(8,128)(2,1)} %bitcast.19, bf16[32,32768]{1,0:T(8,128)(2,1)} %bitcast.18, bf16[64,32]{1,0:T(8,128)(2,1)} %bitcast.21, bf16[2,64,64]{2,1,0:T(8,128)(2,1)} %bitcast.22, ...), custom_call_target="tpu_custom_call" | custom-call | tf_op jit(solution)/shard_map/owner_forward/pallas_call | solution.py:491
  118.8 28.7 %finish.1 = (f32[1,256]{1,0:T(1,128)}, f32[16,32]{1,0:T(8,128)}, f32[1,16]{1,0:T(1,128)}) custom-call(f32[32,2,128]{2,1,0:T(2,128)} %get-tuple-element.9.stats_ref, s32[32,32]{1,0:T(8,128)} %bitcast.23, s32[32,32]{1,0:T(8,128)} %bitcast.24, s32[1,32]{1,0:T(1,128)} %bitcast.28, f32[16,1]{1,0:T(8,128)} %copy.20.prop_out_ref, ...), custom_call_target="tpu_custom_call" | custom-call | tf_op jit(solution)/shard_map/finish/pallas_call | solution.py:524
  147.5 1.2 copy.27
  148.7 1.3 copy.28
  150.0 1.1 copy.29
Async XLA Ops:
  2.9 19.2 %all-to-all-start = ((bf16[4,1,1,32,2048]{4,0,2,1,3:T(4,128)(2,1)}), bf16[4,1,1,32,2048]{4,0,2,1,3:T(4,128)(2,1)S(1)}, u32[]{:S(2)}, u32[]{:S(2)}) async-start(bf16[4,1,1,32,2048]{4,0,2,1,3:T(4,128)(2,1)} %copy.17), calls=%async_computation | async-start | bytes 1048576 | tf_op jit(solution)/shard_map/all_to_all | solution.py:490

commit v4 on v3

--- a/solution.py
+++ b/solution.py
@@ -10,7 +10,8 @@
 GR = 32
 RAY_DEV = 256
 TILE = 1024
-PART = 512
+PART = 256
+SHARES = (0, 128, 384, 640, 896, 1024)
 
 distill_weight = 50.0
 f32 = jnp.float32
@@ -56,6 +57,7 @@
     cells_ref, geom_ref, grid_ref, fine_in_ref, fine_mid_ref, fine_out_ref, prop_in_ref, prop_out_ref,
     kept_ref, back_ref, stats_ref,
     table, even, odd, geo, fine_logit, prop_logit, spacing, even_cells, odd_cells, sems,
+    first_all, mid_all, fine_head, prop_head, even_hold, odd_hold,
 ):
     sources, width = geom_ref.shape[1:]
     tiles_per = width // TILE
@@ -66,32 +68,53 @@
     geo[...] = geom_ref[...].astype(f32)
     lane = lax.broadcasted_iota(jnp.int32, (GR, 128), 1)
 
-    def build(second, block, carry):
+    shifts = (1, GR, GR + 1)
+
+    def block_of(block):
         here = grid_ref[:, pl.ds(pl.multiple_of(block * 128, 128), 128)].astype(f32)
-        after = jnp.minimum(block + 1, cell_blocks - 1)
-        there = grid_ref[:, pl.ds(pl.multiple_of(after * 128, 128), 128)].astype(f32)
-        pieces = [here]
-        for shift in (1, GR, GR + 1):
-            pieces.append(
-                jnp.where(
-                    lane < 128 - shift,
-                    pltpu.roll(here, 128 - shift, 1),
-                    pltpu.roll(there, 128 - shift, 1),
-                )
-            )
-        turned = jnp.transpose(jnp.concatenate(pieces, axis=0))
+        return (here,) + tuple(pltpu.roll(here, 128 - shift, 1) for shift in shifts)
+
+    def build(second, block, here):
+        there = block_of(jnp.minimum(block + 1, cell_blocks - 1))
+        pieces = [here[0]]
+        for index, shift in enumerate(shifts):
+            pieces.append(jnp.where(lane < 128 - shift, here[index + 1], there[index + 1]))
+        turned = jnp.transpose(jnp.concatenate(pieces, axis=0).astype(bf16)).astype(f32)
         table[pl.ds(pl.multiple_of(block * 256, 256), 128, stride=2), :] = turned
         if second:
             earlier = pl.multiple_of((block - GR * GR // 128) * 256, 256)
             table[pl.ds(earlier + 1, 128, stride=2), :] = turned
-        return carry
+        return there
 
     slab = GR * GR // 128
-    lax.fori_loop(0, slab, functools.partial(build, False), 0)
-    lax.fori_loop(slab, cell_blocks, functools.partial(build, True), 0, unroll=2)
-
-    first = jnp.concatenate([fine_in_ref[...], prop_in_ref[...]], axis=0)
+    state = lax.fori_loop(0, slab, functools.partial(build, False), block_of(0))
+    lax.fori_loop(slab, cell_blocks, functools.partial(build, True), state, unroll=4)
+
     hidden = fine_in_ref.shape[0]
+    groups = TILE // PART
+
+    def diagonal(weights):
+        rows, columns = weights.shape
+        wide = jnp.concatenate([weights.astype(f32)] * groups, axis=1)
+        tall = jnp.concatenate([wide] * groups, axis=0)
+        row = lax.broadcasted_iota(jnp.int32, tall.shape, 0) // rows
+        column = lax.broadcasted_iota(jnp.int32, tall.shape, 1) // columns
+        return jnp.where(row == column, tall, 0.0)
+
+    def heads(weights):
+        columns = weights.shape[1]
+        wide = jnp.concatenate([weights.astype(f32)] * groups, axis=1)
+        tall = jnp.broadcast_to(wide, (16, wide.shape[1]))
+        row = lax.broadcasted_iota(jnp.int32, tall.shape, 0)
+        column = lax.broadcasted_iota(jnp.int32, tall.shape, 1) // columns
+        return jnp.where(row == column, tall, 0.0).astype(bf16)
+
+    first_all[pl.ds(0, groups * hidden), :] = diagonal(fine_in_ref[...]).astype(bf16)
+    first_all[pl.ds(groups * hidden, groups * 16), :] = diagonal(prop_in_ref[...]).astype(bf16)
+    for layer in range(fine_mid_ref.shape[0]):
+        mid_all[layer] = diagonal(fine_mid_ref[layer]).astype(bf16)
+    fine_head[...] = heads(fine_out_ref[...])
+    prop_head[...] = heads(prop_out_ref[...])
     eye = (
         lax.broadcasted_iota(jnp.int32, (256, 256), 0)
         == lax.broadcasted_iota(jnp.int32, (256, 256), 1)
@@ -106,67 +129,87 @@
             cell = pl.multiple_of(indices[j], 2)
             low[pl.ds(2 * j, 2), :] = table[pl.ds(cell, 2), :]
 
-    def evaluate(tile, low, part):
+    def interpolate(tile, low, hold):
         source = tile // tiles_per
         first_lane = (tile % tiles_per) * TILE
-        if True:
-            lanes = pl.ds(pl.multiple_of(first_lane + part * PART, PART), PART)
-            start = 2 * part * PART
-            rows = jnp.concatenate(
-                [
-                    low[pl.ds(start, PART, stride=2), :],
-                    low[pl.ds(start + 1, PART, stride=2), :],
-                ],
-                axis=1,
+        places = [
+            pl.ds(pl.multiple_of(first_lane + part * PART, PART), PART) for part in range(groups)
+        ]
+        waiting = []
+        for part in range(groups + 1):
+            if part < groups:
+                start = 2 * part * PART
+                rows = jnp.concatenate(
+                    [
+                        low[pl.ds(start, PART, stride=2), :],
+                        low[pl.ds(start + 1, PART, stride=2), :],
+                    ],
+                    axis=1,
+                ).astype(bf16)
+                waiting.append(
+                    lax.dot_general(eye, rows, LANES_BOTH, preferred_element_type=f32)
+                )
+            if part > 0:
+                lanes = places[part - 1]
+                turned = waiting[part - 1]
+                offsets = [geo[axis, pl.ds(source, 1), lanes] for axis in range(3)]
+                factors = [[1.0 - value, value] for value in offsets]
+                summed = jnp.zeros((32, PART), f32)
+                for corner in range(8):
+                    factor = (
+                        factors[0][corner // 4]
+                        * factors[1][corner // 2 % 2]
+                        * factors[2][corner % 2]
+                    )
+                    summed = summed + turned[corner * 32 : (corner + 1) * 32] * factor
+                features = summed.astype(bf16)
+                kept_ref[source, pl.ds(0, 32), lanes] = features
+                hold[pl.ds((part - 1) * 32, 32), :] = features
+            yield
+
+    def networks(tile, hold):
+        source = tile // tiles_per
+        first_lane = (tile % tiles_per) * TILE
+        places = [
+            pl.ds(pl.multiple_of(first_lane + part * PART, PART), PART) for part in range(groups)
+        ]
+        both = jnp.maximum(
+            jnp.dot(first_all[...], hold[...], preferred_element_type=f32), 0.0
+        ).astype(bf16)
+        fine_hidden = both[: groups * hidden]
+        prop_hidden = both[groups * hidden :]
+        for part in range(groups):
+            kept_ref[source, pl.ds(32, 16), places[part]] = prop_hidden[
+                part * 16 : (part + 1) * 16
+            ]
+        yield
+        for layer in range(fine_mid_ref.shape[0]):
+            fine_hidden = jnp.maximum(
+                jnp.dot(mid_all[layer], fine_hidden, preferred_element_type=f32), 0.0
             ).astype(bf16)
-            turned = lax.dot_general(eye, rows, LANES_BOTH, preferred_element_type=f32)
             yield
-            offsets = [geo[axis, pl.ds(source, 1), lanes] for axis in range(3)]
-            factors = [[1.0 - value, value] for value in offsets]
-            summed = jnp.zeros((32, PART), f32)
-            for corner in range(8):
-                factor = (
-                    factors[0][corner // 4]
-                    * factors[1][corner // 2 % 2]
-                    * factors[2][corner % 2]
-                )
-                summed = summed + turned[corner * 32 : (corner + 1) * 32] * factor
-            features = summed.astype(bf16)
-            kept_ref[source, pl.ds(0, 32), lanes] = features
-            yield
-            both = jnp.maximum(
-                jnp.dot(first, features, preferred_element_type=f32), 0.0
-            ).astype(bf16)
-            prop_hidden = both[hidden:]
-            fine_hidden = both[:hidden]
-            kept_ref[source, pl.ds(32, 16), lanes] = prop_hidden
-            yield
-            for layer in range(fine_mid_ref.shape[0]):
-                fine_hidden = jnp.maximum(
-                    jnp.dot(fine_mid_ref[layer], fine_hidden, preferred_element_type=f32), 0.0
-                ).astype(bf16)
-                yield
-            fine = jnp.dot(fine_out_ref[...], fine_hidden, preferred_element_type=f32)
-            prop = jnp.dot(prop_out_ref[...], prop_hidden, preferred_element_type=f32)
-            gap = geo[3, pl.ds(source, 1), lanes]
+        fine = jnp.dot(fine_head[...], fine_hidden, preferred_element_type=f32)
+        prop = jnp.dot(prop_head[...], prop_hidden, preferred_element_type=f32)
+        for part in range(groups):
+            gap = geo[3, pl.ds(source, 1), places[part]]
             for piece in range(PART // 128):
                 row = pl.ds(tile * (TILE // 128) + (part * PART) // 128 + piece, 1)
                 cut = slice(piece * 128, (piece + 1) * 128)
-                fine_logit[row, :] = fine[:, cut]
-                prop_logit[row, :] = prop[:, cut]
+                fine_logit[row, :] = fine[part : part + 1, cut]
+                prop_logit[row, :] = prop[part : part + 1, cut]
                 spacing[row, :] = gap[:, cut]
-            yield
-
-    def weave(indices, into, tile, out_of):
-        parts = TILE // PART
-        stages = 4 + fine_mid_ref.shape[0]
-        slots = stages + parts - 1
-        running = [evaluate(tile, out_of, part) for part in range(parts)]
+        yield
+
+    def weave(indices, into, tile, out_of, hold_now, hold_last):
+        slots = groups + 1
+        ahead = networks(jnp.maximum(tile - 1, 0), hold_last)
+        now = interpolate(tile, out_of, hold_now)
         for slot in range(slots):
-            for part in range(parts):
-                if 0 <= slot - part < stages:
-                    next(running[part])
-            gather(indices, into, slot * TILE // slots, (slot + 1) * TILE // slots)
+            gather(indices, into, SHARES[slot], SHARES[slot + 1])
+            next(ahead, None)
+            next(now, None)
+        for unused in ahead:
+            pass
 
     fetch(0, even_cells, sems.at[0]).start()
     fetch(1, odd_cells, sems.at[1]).start()
@@ -178,18 +221,20 @@
         def _():
             fetch(tile + 2, even_cells, sems.at[0]).start()
             fetch(tile + 1, odd_cells, sems.at[1]).wait()
-            weave(odd_cells, odd, tile, even)
+            weave(odd_cells, odd, tile, even, even_hold, odd_hold)
 
         @pl.when(tile % 2 == 1)
         def _():
             fetch(tile + 2, odd_cells, sems.at[1]).start()
             fetch(tile + 1, even_cells, sems.at[0]).wait()
-            weave(even_cells, even, tile, odd)
+            weave(even_cells, even, tile, odd, odd_hold, even_hold)
 
         return carry
 
     lax.fori_loop(0, tile_total, step, 0)
     fetch(tile_total, odd_cells, sems.at[1]).wait()
+    for unused in networks(tile_total - 1, odd_hold):
+        pass
 
     gap = spacing[...]
     prop_raw = prop_logit[...]
@@ -508,6 +553,12 @@
             pltpu.SMEM((TILE,), jnp.int32),
             pltpu.SMEM((TILE,), jnp.int32),
             pltpu.SemaphoreType.DMA((2,)),
+            pltpu.VMEM((TILE // PART * 80, TILE // PART * 32), bf16),
+            pltpu.VMEM((fine_mid.shape[1], TILE // PART * 64, TILE // PART * 64), bf16),
+            pltpu.VMEM((16, TILE // PART * 64), bf16),
+            pltpu.VMEM((16, TILE // PART * 16), bf16),
+            pltpu.VMEM((TILE // PART * 32, PART), bf16),
+            pltpu.VMEM((TILE // PART * 32, PART), bf16),
         ],
         compiler_params=params,
         name="owner_forward",

time: 152 us -> 127 us (0.84)
  Pallas kernels: 124 us -> 99.3 us
    pallas_call x1, Pallas kernels: 95.7 us -> 70.7 us  [on_device(): pl.pallas_call(owner_kernel, out_shape=(jax.ShapeDtypeStruct((sources, 48...]
  transfers between devices with their start and end apart: 1 -> 1, of which waited for: 1 -> 1; matrix products, arithmetic and copies ran while one was open for 3% -> 4% of each run, Pallas kernels for 0% -> 0%
where the time goes in v4:
time: 127 us; the launch traced here: 126 us
  Pallas kernels  99.3 us (78%)
  local copies, waits for them, and re-layouts  9.73 us (8%)
  starting transfers between devices  7.4 us (6%)
  waiting for transfers between devices  7.31 us (6%)
  other arithmetic  1.63 us (1%)
    pallas_call x1, Pallas kernels, on_device(): pl.pallas_call(owner_kernel, out_shape=(jax.ShapeDtypeStruct((sources, 48...  70.7 us
    pallas_call x1, Pallas kernels, on_device(): pl.pallas_call(finish_kernel, out_shape=(jax.ShapeDtypeStruct((1, RAY_DEV...  28.6 us
    unnamed x6, local copies, waits for them, and re-layouts  7.98 us
    all_to_all x1, starting transfers between devices, on_device(): lax.all_to_all(sample_geometry, 'dom', split_axis=3, concat_axis=3, tiled...  7.4 us
    all_to_all x1, waiting for transfers between devices, on_device(): lax.all_to_all(sample_geometry, 'dom', split_axis=3, concat_axis=3, tiled...  7.31 us
  transfers between devices with their start and end apart: 1, of which 1 were waited for; matrix products, arithmetic and copies ran while one was open for 4% of the time, Pallas kernels for 0%

profile of v4, /device:TPU:0, one launch (start us, length us, event | category | flops | bytes accessed | tf_op | source)
XLA Modules:
  0.0 126.0 jit_solution(16728443886855327086)
XLA Ops:
  0.6 2.2 %copy.17 = bf16[4,1,1,32,2048]{4,0,2,1,3:T(4,128)(2,1)} copy(bf16[4,1,1,32,2048]{4,3,2,1,0:T(8,128)(2,1)} %param.18) | data formatting | bytes 1048576 | tf_op args[7]
  2.9 7.4 %all-to-all-start = ((bf16[4,1,1,32,2048]{4,0,2,1,3:T(4,128)(2,1)}), bf16[4,1,1,32,2048]{4,0,2,1,3:T(4,128)(2,1)S(1)}, u32[]{:S(2)}, u32[]{:S(2)}) async-start(bf16[4,1,1,32,2048]{4,0,2,1,3:T(4,128)(2,1)} %copy.17), calls=%async_computation | async-start | bytes 1048576 | tf_op jit(solution)/shard_map/all_to_all | solution.py:535
  10.3 1.0 multiply_bitcast_fusion
  11.3 0.8 copy.21
  12.0 1.4 %copy.19 = bf16[1,64,32]{2,1,0:T(8,128)(2,1)} copy(bf16[1,64,32]{1,2,0:T(8,128)(2,1)} %param.12) | data formatting | bytes 8192 | tf_op args[1]
  13.4 0.7 bitcast_convert_fusion
  14.0 0.7 copy.20.prop_out_ref
  14.7 7.3 %all-to-all-done = bf16[4,1,1,32,2048]{4,0,2,1,3:T(4,128)(2,1)S(1)} async-done(((bf16[4,1,1,32,2048]{4,0,2,1,3:T(4,128)(2,1)}), bf16[4,1,1,32,2048]{4,0,2,1,3:T(4,128)(2,1)S(1)}, u32[]{:S(2)}, u32[]{:S(2)}) %all-to-all-start) | async-done | bytes 524320 | tf_op jit(solution)/shard_map/all_to_all | solution.py:535
  22.0 1.1 copy.23
  23.1 70.7 %owner_forward.1 = (bf16[32,48,2048]{2,1,0:T(8,128)(2,1)}, f32[4,512,128]{2,1,0:T(8,128)}, f32[32,2,128]{2,1,0:T(2,128)}) custom-call(s32[65536]{0:T(1024)} %bitcast.20, bf16[4,32,2048]{2,1,0:T(8,128)(2,1)} %bitcast.19, bf16[32,32768]{1,0:T(8,128)(2,1)} %bitcast.18, bf16[64,32]{1,0:T(8,128)(2,1)} %bitcast.21, bf16[2,64,64]{2,1,0:T(8,128)(2,1)} %bitcast.22, ...), custom_call_target="tpu_custom_call" | custom-call | tf_op jit(solution)/shard_map/owner_forward/pallas_call | solution.py:536
  93.8 28.6 %finish.1 = (f32[1,256]{1,0:T(1,128)}, f32[16,32]{1,0:T(8,128)}, f32[1,16]{1,0:T(1,128)}) custom-call(f32[32,2,128]{2,1,0:T(2,128)} %get-tuple-element.9.stats_ref, s32[32,32]{1,0:T(8,128)} %bitcast.23, s32[32,32]{1,0:T(8,128)} %bitcast.24, s32[1,32]{1,0:T(1,128)} %bitcast.28, f32[16,1]{1,0:T(8,128)} %copy.20.prop_out_ref, ...), custom_call_target="tpu_custom_call" | custom-call | tf_op jit(solution)/shard_map/finish/pallas_call | solution.py:575
  122.4 1.2 copy.27
  123.6 1.3 %copy.28 = f32[1,16,32]{2,1,0:T(8,128)} copy(f32[1,16,32]{2,1,0:T(8,128)} %bitcast.25) | data formatting | bytes 4096
  124.9 1.1 copy.29
Async XLA Ops:
  2.9 19.2 %all-to-all-start = ((bf16[4,1,1,32,2048]{4,0,2,1,3:T(4,128)(2,1)}), bf16[4,1,1,32,2048]{4,0,2,1,3:T(4,128)(2,1)S(1)}, u32[]{:S(2)}, u32[]{:S(2)}) async-start(bf16[4,1,1,32,2048]{4,0,2,1,3:T(4,128)(2,1)} %copy.17), calls=%async_computation | async-start | bytes 1048576 | tf_op jit(solution)/shard_map/all_to_all | solution.py:535

commit v5 on v4

--- a/solution.py
+++ b/solution.py
@@ -10,6 +10,7 @@
 GR = 32
 RAY_DEV = 256
 TILE = 1024
+PIECES = 4
 PART = 256
 SHARES = (0, 128, 384, 640, 896, 1024)
 
@@ -53,42 +54,92 @@
     return within + jnp.where(edge, moved(running, 1, 0), 0.0), total
 
 
-def owner_kernel(
-    cells_ref, geom_ref, grid_ref, fine_in_ref, fine_mid_ref, fine_out_ref, prop_in_ref, prop_out_ref,
-    kept_ref, back_ref, stats_ref,
-    table, even, odd, geo, fine_logit, prop_logit, spacing, even_cells, odd_cells, sems,
-    first_all, mid_all, fine_head, prop_head, even_hold, odd_hold,
-):
-    sources, width = geom_ref.shape[1:]
-    tiles_per = width // TILE
-    tile_total = sources * tiles_per
+def scatter_kernel(geom_ref, grid_ref, geo_ref, table_hbm, arrived, table, send, recv, local):
+    sources = geom_ref.shape[0]
     cell_blocks = grid_ref.shape[1] // 128
-    rows_per = width // 128
-
-    geo[...] = geom_ref[...].astype(f32)
+    me, replica = lax.axis_index("dom"), lax.axis_index("rep")
+    barrier = pltpu.get_barrier_semaphore()
+
+    def greet(step, carry):
+        peer = lax.rem(me + step, sources)
+        pl.semaphore_signal(barrier, inc=1, device_id=(peer, replica), device_id_type=MESH)
+        return carry
+
+    lax.fori_loop(1, sources, greet, 0)
+    pl.semaphore_wait(barrier, sources - 1)
+
+    def copy(step):
+        peer = lax.rem(me + step, sources)
+        return pltpu.make_async_remote_copy(
+            src_ref=geom_ref.at[peer],
+            dst_ref=arrived.at[me],
+            send_sem=send.at[step],
+            recv_sem=recv.at[step],
+            device_id=(peer, replica),
+            device_id_type=MESH,
+        )
+
+    def start(step, carry):
+        copy(step).start()
+        return carry
+
+    def finish(step, carry):
+        copy(step).wait()
+        return carry
+
+    lax.fori_loop(1, sources, start, 0)
+    own = pltpu.make_async_copy(geom_ref.at[me], arrived.at[me], local.at[PIECES])
+    own.start()
+
     lane = lax.broadcasted_iota(jnp.int32, (GR, 128), 1)
-
     shifts = (1, GR, GR + 1)
 
     def block_of(block):
         here = grid_ref[:, pl.ds(pl.multiple_of(block * 128, 128), 128)].astype(f32)
         return (here,) + tuple(pltpu.roll(here, 128 - shift, 1) for shift in shifts)
 
-    def build(second, block, here):
+    def build(block, here):
         there = block_of(jnp.minimum(block + 1, cell_blocks - 1))
         pieces = [here[0]]
         for index, shift in enumerate(shifts):
             pieces.append(jnp.where(lane < 128 - shift, here[index + 1], there[index + 1]))
-        turned = jnp.transpose(jnp.concatenate(pieces, axis=0).astype(bf16)).astype(f32)
-        table[pl.ds(pl.multiple_of(block * 256, 256), 128, stride=2), :] = turned
-        if second:
-            earlier = pl.multiple_of((block - GR * GR // 128) * 256, 256)
-            table[pl.ds(earlier + 1, 128, stride=2), :] = turned
+        table[pl.ds(pl.multiple_of(block * 128, 128), 128), :] = jnp.transpose(
+            jnp.concatenate(pieces, axis=0).astype(bf16)
+        )
         return there
 
-    slab = GR * GR // 128
-    state = lax.fori_loop(0, slab, functools.partial(build, False), block_of(0))
-    lax.fori_loop(slab, cell_blocks, functools.partial(build, True), state, unroll=4)
+    state = block_of(0)
+    per_piece = cell_blocks // PIECES
+    for piece in range(PIECES):
+        state = lax.fori_loop(
+            piece * per_piece, (piece + 1) * per_piece, build, state, unroll=4
+        )
+        table_piece(table, table_hbm, local, piece).start()
+    own.wait()
+    lax.fori_loop(1, sources, finish, 0)
+    geo_ref[...] = arrived[...].astype(f32)
+    for piece in range(PIECES):
+        table_piece(table, table_hbm, local, piece).wait()
+
+
+def table_piece(source, target, sems, piece):
+    height = source.shape[0] // PIECES
+    rows = pl.ds(piece * height, height)
+    return pltpu.make_async_copy(source.at[rows], target.at[rows], sems.at[piece])
+
+
+def owner_kernel(
+    cells_ref, geo, table_hbm, fine_in_ref, fine_mid_ref, fine_out_ref, prop_in_ref, prop_out_ref,
+    kept_hbm, back_ref, stats_ref,
+    kept_ref, kept_sems, narrow, table, even, odd, fine_logit, prop_logit, spacing, even_cells, odd_cells, sems,
+    first_all, mid_all, fine_head, prop_head, even_hold, odd_hold,
+):
+    sources, rows_kept, width = kept_ref.shape
+    tiles_per = width // TILE
+    tile_total = sources * tiles_per
+    rows_per = width // 128
+    for piece in range(PIECES):
+        table_piece(table_hbm, narrow, kept_sems, piece).start()
 
     hidden = fine_in_ref.shape[0]
     groups = TILE // PART
@@ -119,6 +170,31 @@
         lax.broadcasted_iota(jnp.int32, (256, 256), 0)
         == lax.broadcasted_iota(jnp.int32, (256, 256), 1)
     ).astype(f32).astype(bf16)
+
+    cell_blocks = table_hbm.shape[0] // 128
+    slab = GR * GR // 128
+    per_piece = cell_blocks // PIECES
+
+    def widen(second, block, carry):
+        rows = narrow[pl.ds(pl.multiple_of(block * 128, 128), 128), :].astype(f32)
+        table[pl.ds(pl.multiple_of(block * 256, 256), 128, stride=2), :] = rows
+        if second:
+            earlier = pl.multiple_of((block - slab) * 256, 256)
+            table[pl.ds(earlier + 1, 128, stride=2), :] = rows
+        return carry
+
+    for piece in range(PIECES):
+        table_piece(table_hbm, narrow, kept_sems, piece).wait()
+        low = piece * per_piece
+        if piece == 0:
+            lax.fori_loop(0, slab, functools.partial(widen, False), 0)
+            low = slab
+        lax.fori_loop(low, (piece + 1) * per_piece, functools.partial(widen, True), 0, unroll=4)
+
+    def save(source):
+        return pltpu.make_async_copy(
+            kept_ref.at[source], kept_hbm.at[source], kept_sems.at[source]
+        )
 
     def fetch(tile, indices, sem):
         start = pl.multiple_of(jnp.minimum(tile, tile_total - 1) * TILE, TILE)
@@ -152,7 +228,17 @@
             if part > 0:
                 lanes = places[part - 1]
                 turned = waiting[part - 1]
-                offsets = [geo[axis, pl.ds(source, 1), lanes] for axis in range(3)]
+                place = tile % tiles_per * (TILE // 128) + (part - 1) * (PART // 128)
+                offsets = [
+                    jnp.concatenate(
+                        [
+                            geo[source, pl.ds(axis * rows_per + place + piece, 1), :]
+                            for piece in range(PART // 128)
+                        ],
+                        axis=1,
+                    )
+                    for axis in range(3)
+                ]
                 factors = [[1.0 - value, value] for value in offsets]
                 summed = jnp.zeros((32, PART), f32)
                 for corner in range(8):
@@ -188,16 +274,21 @@
                 jnp.dot(mid_all[layer], fine_hidden, preferred_element_type=f32), 0.0
             ).astype(bf16)
             yield
+        spacing[pl.ds(pl.multiple_of(tile * (TILE // 128), 8), TILE // 128), :] = geo[
+            source,
+            pl.ds(
+                pl.multiple_of(3 * rows_per + tile % tiles_per * (TILE // 128), 8), TILE // 128
+            ),
+            :,
+        ]
         fine = jnp.dot(fine_head[...], fine_hidden, preferred_element_type=f32)
         prop = jnp.dot(prop_head[...], prop_hidden, preferred_element_type=f32)
         for part in range(groups):
-            gap = geo[3, pl.ds(source, 1), places[part]]
             for piece in range(PART // 128):
                 row = pl.ds(tile * (TILE // 128) + (part * PART) // 128 + piece, 1)
                 cut = slice(piece * 128, (piece + 1) * 128)
                 fine_logit[row, :] = fine[part : part + 1, cut]
                 prop_logit[row, :] = prop[part : part + 1, cut]
-                spacing[row, :] = gap[:, cut]
         yield
 
     def weave(indices, into, tile, out_of, hold_now, hold_last):
@@ -217,6 +308,10 @@
     gather(even_cells, even)
 
     def step(tile, carry):
+        @pl.when((tile % 2 == 0) & (tile >= 4))
+        def _():
+            save(tile // 2 - 2).start()
+
         @pl.when(tile % 2 == 0)
         def _():
             fetch(tile + 2, even_cells, sems.at[0]).start()
@@ -235,6 +330,9 @@
     fetch(tile_total, odd_cells, sems.at[1]).wait()
     for unused in networks(tile_total - 1, odd_hold):
         pass
+
+    save(sources - 2).start()
+    save(sources - 1).start()
 
     gap = spacing[...]
     prop_raw = prop_logit[...]
@@ -265,6 +363,12 @@
     )
     stats_ref[:, 1, :] = log_fine
 
+    def saved(source, carry):
+        save(source).wait()
+        return carry
+
+    lax.fori_loop(0, sources, saved, 0)
+
 
 def split_three(value):
     high = value.astype(bf16)
@@ -276,7 +380,7 @@
 
 def finish_kernel(
     stats_ref, ray_ref, rank_ref, count_ref, prop_out_ref, back_hbm, kept_hbm,
-    loss_ref, in_ref, out_ref,
+    result_ref,
     stats_in, factors_out, factors_in, grads_in, flat, ahead, logit_grad, left, back_ref, kept_ref,
     stats_send, stats_recv, factors_send, factors_recv, grads_send, grads_recv, local,
 ):
@@ -447,7 +551,9 @@
         ray_loss = ray_loss + jnp.dot(
             losses[:, chunk * 128 : (chunk + 1) * 128], mask, preferred_element_type=f32
         )
-    loss_ref[...] = 0.5 * distill_weight * (ray_loss[0:1] + ray_loss[1:2] + ray_loss[2:3])
+    ray_loss = 0.5 * distill_weight * (ray_loss[0:1] + ray_loss[1:2] + ray_loss[2:3])
+    for index in range(RAY_DEV // 128):
+        result_ref[pl.ds(32 + index, 1), :] = ray_loss[:, index * 128 : (index + 1) * 128]
 
     load_back.wait()
     load_kept.wait()
@@ -503,8 +609,8 @@
     summed = grads_in[0]
     for index in range(1, replicas):
         summed = summed + grads_in[index]
-    in_ref[...] = summed[0:16, 0:32] * prop_out_ref[...]
-    out_ref[...] = summed[16:17, 32:48]
+    result_ref[pl.ds(0, 16), :] = summed[0:16] * prop_out_ref[...]
+    result_ref[pl.ds(16, 16), :] = summed[16:32]
 
 
 def vmem():
@@ -530,9 +636,33 @@
     rows_all = sources * width // 128
     slots = sources * capacity
     cell_total = feature_grid.shape[2]
-    params = pltpu.CompilerParams(vmem_limit_bytes=58 * 2**20)
-
-    arrived = lax.all_to_all(sample_geometry, "dom", split_axis=3, concat_axis=3, tiled=True)
+    params = pltpu.CompilerParams(vmem_limit_bytes=60 * 2**20)
+
+    by_part = (
+        sample_geometry.reshape(4, sources, width)
+        .transpose(1, 0, 2)
+        .reshape(sources, 4 * width // 128, 128)
+    )
+    geometry, corners = pl.pallas_call(
+        scatter_kernel,
+        out_shape=(
+            jax.ShapeDtypeStruct(by_part.shape, f32),
+            jax.ShapeDtypeStruct((cell_total, 128), bf16),
+        ),
+        in_specs=[vmem()] * 2,
+        out_specs=(vmem(), pl.BlockSpec(memory_space=pl.ANY)),
+        scratch_shapes=[
+            pltpu.VMEM(by_part.shape, bf16),
+            pltpu.VMEM((cell_total, 128), bf16),
+            pltpu.SemaphoreType.DMA((sources,)),
+            pltpu.SemaphoreType.DMA((sources,)),
+            pltpu.SemaphoreType.DMA((PIECES + 1,)),
+        ],
+        compiler_params=pltpu.CompilerParams(
+            vmem_limit_bytes=40 * 2**20, collective_id=1, has_side_effects=True
+        ),
+        name="scatter_geometry",
+    )(by_part, feature_grid[0])
     kept, back, stats = pl.pallas_call(
         owner_kernel,
         out_shape=(
@@ -540,13 +670,16 @@
             jax.ShapeDtypeStruct((4, rows_all, 128), f32),
             jax.ShapeDtypeStruct((sources, 2, 128), f32),
         ),
-        in_specs=[pl.BlockSpec(memory_space=pl.ANY)] + [vmem()] * 7,
-        out_specs=(vmem(), vmem(), vmem()),
+        in_specs=[pl.BlockSpec(memory_space=pl.ANY), vmem(), pl.BlockSpec(memory_space=pl.ANY)]
+        + [vmem()] * 5,
+        out_specs=(pl.BlockSpec(memory_space=pl.ANY), vmem(), vmem()),
         scratch_shapes=[
+            pltpu.VMEM((sources, 48, width), bf16),
+            pltpu.SemaphoreType.DMA((sources,)),
+            pltpu.VMEM((cell_total, 128), bf16),
             pltpu.VMEM((2 * cell_total, 128), f32),
             pltpu.VMEM((2 * TILE, 128), f32),
             pltpu.VMEM((2 * TILE, 128), f32),
-            pltpu.VMEM((4, sources, width), f32),
             pltpu.VMEM((rows_all, 128), f32),
             pltpu.VMEM((rows_all, 128), f32),
             pltpu.VMEM((rows_all, 128), f32),
@@ -564,23 +697,19 @@
         name="owner_forward",
     )(
         (sample_cells * 2).reshape(sources * width),
-        arrived.reshape(4, sources, width),
-        feature_grid[0],
+        geometry,
+        corners,
         fine_in[0],
         fine_mid[0],
         fine_out,
         prop_in[0],
         prop_out,
     )
-    ray_loss, in_sum, out_sum = pl.pallas_call(
+    result = pl.pallas_call(
         finish_kernel,
-        out_shape=(
-            jax.ShapeDtypeStruct((1, RAY_DEV), f32),
-            jax.ShapeDtypeStruct((16, 32), f32),
-            jax.ShapeDtypeStruct((1, 16), f32),
-        ),
+        out_shape=jax.ShapeDtypeStruct((32 + RAY_DEV // 128, 128), f32),
         in_specs=[vmem()] * 5 + [pl.BlockSpec(memory_space=pl.ANY)] * 2,
-        out_specs=(vmem(), vmem(), vmem()),
+        out_specs=vmem(),
         scratch_shapes=[
             pltpu.VMEM((sources, 2, 128), f32),
             pltpu.VMEM((sources, 1, 128), f32),
@@ -613,7 +742,7 @@
         back,
         kept,
     )
-    return (ray_loss.reshape(1, 1, -1), in_sum[None], out_sum)
+    return (result[32:].reshape(1, 1, RAY_DEV), result[None, 0:16, 0:32], result[16:17, 32:48])
 
 
 def solution(mesh):

time: 127 us -> 126 us (level)
  Pallas kernels: 99.3 us -> 109 us
  starting transfers between devices: 7.4 us -> 0 us
  waiting for transfers between devices: 7.31 us -> 0 us
  local copies, waits for them, and re-layouts: 9.73 us -> 14.2 us
    pallas_call x1 -> x2, Pallas kernels: 28.6 us -> 46.8 us  [the longest x1 28.8 us: on_device(): pl.pallas_call(finish_kernel, out_shape=jax.ShapeDtypeStruct((32 + RAY_DE...]
    pallas_call x1, Pallas kernels: 70.7 us -> 62.3 us  [on_device(): pl.pallas_call(owner_kernel, out_shape=(jax.ShapeDtypeStruct((sources, 48...]
    all_to_all x1 -> x0, starting transfers between devices: 7.4 us -> none  [on_device(): lax.all_to_all(sample_geometry, 'dom', split_axis=3, concat_axis=3, tiled...]
    all_to_all x1 -> x0, waiting for transfers between devices: 7.31 us -> none  [on_device(): lax.all_to_all(sample_geometry, 'dom', split_axis=3, concat_axis=3, tiled...]
    slice x0 -> x2, local copies, waits for them, and re-layouts: none -> 2.51 us  [the longest x1 1.26 us: on_device(): result[16:17, 32:48]]
    transpose x0 -> x1, local copies, waits for them, and re-layouts: none -> 1.45 us  [on_device(): by_part = sample_geometry.reshape(4, sources, width).transpose(1, 0, 2).r...]
    broadcast_in_dim x0 -> x1, local copies, waits for them, and re-layouts: none -> 1.3 us  [on_device(): result[None, 0:16, 0:32]]
    unnamed x6 -> x10, local copies, waits for them, and re-layouts: 7.98 us -> 7.93 us
  transfers between devices with their start and end apart: 1 -> 0, of which waited for: 1 -> 0; matrix products, arithmetic and copies ran while one was open for 4% -> 0% of each run, Pallas kernels for 0% -> 0%
where the time goes in v5:
time: 126 us; the launch traced here: 125 us
  Pallas kernels  109 us (87%)
  local copies, waits for them, and re-layouts  14.2 us (11%)
    pallas_call x1, Pallas kernels, on_device(): pl.pallas_call(owner_kernel, out_shape=(jax.ShapeDtypeStruct((sources, 48...  62.3 us
    pallas_call x1, Pallas kernels, on_device(): pl.pallas_call(finish_kernel, out_shape=jax.ShapeDtypeStruct((32 + RAY_DE...  28.8 us
    pallas_call x1, Pallas kernels, on_device(): pl.pallas_call(scatter_kernel, out_shape=(jax.ShapeDtypeStruct(by_part.sh...  18 us
    unnamed x10, local copies, waits for them, and re-layouts  7.93 us

profile of v5, /device:TPU:0, one launch (start us, length us, event | category | flops | bytes accessed | tf_op | source)
XLA Modules:
  0.0 125.0 jit_solution(6229832219006526517)
XLA Ops:
  0.6 1.4 %copy.14 = bf16[32,4,2048]{2,1,0:T(4,128)(2,1)S(1)} copy(bf16[32,4,2048]{2,0,1:T(8,128)(2,1)} %bitcast.21) | data formatting | bytes 1048576 | tf_op jit(solution)/shard_map/transpose | solution.py:643
  2.1 0.3 reshape.32.geom_ref
  2.4 0.0 copy-start.1
  2.4 1.6 %copy-done.1 = bf16[1,32,32768]{2,1,0:T(8,128)(2,1)S(1)} copy-done((bf16[1,32,32768]{2,1,0:T(8,128)(2,1)S(1)}, bf16[1,32,32768]{2,1,0:T(8,128)(2,1)}, u32[]{:S(2)}) %copy-start.1) | copy-done | bytes 2097176
  4.0 0.0 copy-start.3
  4.0 18.0 %scatter_geometry.1 = (f32[32,64,128]{2,1,0:T(8,128)S(1)}, bf16[32768,128]{1,0:T(8,128)(2,1)S(1)}) custom-call(bf16[32,64,128]{2,1,0:T(8,128)(2,1)S(1)} %reshape.32.geom_ref, bf16[32,32768]{1,0:T(8,128)(2,1)S(1)} %bitcast.19), custom_call_target="tpu_custom_call" | custom-call | tf_op jit(solution)/shard_map/scatter_geometry/pallas_call | solution.py:646
  22.0 0.0 copy-start
  22.0 3.2 %copy-done = bf16[32768,128]{1,0:T(8,128)(2,1)} copy-done((bf16[32768,128]{1,0:T(8,128)(2,1)}, bf16[32768,128]{1,0:T(8,128)(2,1)S(1)}, u32[]{:S(2)}) %copy-start) | copy-done | bytes 8388632
  25.2 0.0 copy-start.2
  25.2 1.0 copy-done.2
  26.2 1.0 multiply_bitcast_fusion
  27.2 0.8 copy.17
  28.0 1.4 %copy.15 = bf16[1,64,32]{2,1,0:T(8,128)(2,1)} copy(bf16[1,64,32]{1,2,0:T(8,128)(2,1)} %param.12) | data formatting | bytes 8192 | tf_op args[1]
  29.3 62.3 %owner_forward.1 = (bf16[32,48,2048]{2,1,0:T(8,128)(2,1)}, f32[4,512,128]{2,1,0:T(8,128)}, f32[32,2,128]{2,1,0:T(2,128)}) custom-call(s32[65536]{0:T(1024)} %bitcast.20, f32[32,64,128]{2,1,0:T(8,128)} %copy-done.2, bf16[32768,128]{1,0:T(8,128)(2,1)} %copy-done, bf16[64,32]{1,0:T(8,128)(2,1)} %bitcast.22, bf16[2,64,64]{2,1,0:T(8,128)(2,1)} %bitcast.23, ...), custom_call_target="tpu_custom_call" | custom-call | tf_op jit(solution)/shard_map/owner_forward/pallas_call | solution.py:666
  91.7 0.0 copy-done.3
  91.7 0.7 copy.16.prop_out_ref
  92.4 28.8 %finish.1 = f32[34,128]{1,0:T(8,128)} custom-call(f32[32,2,128]{2,1,0:T(2,128)} %get-tuple-element.10.stats_ref, s32[32,32]{1,0:T(8,128)} %bitcast.24, s32[32,32]{1,0:T(8,128)} %bitcast.25, s32[1,32]{1,0:T(1,128)} %bitcast.28, f32[16,1]{1,0:T(8,128)} %copy.16.prop_out_ref, f32[4,512,128]{2,1,0:T(8,128)} %get-tuple-element.11.back_hbm, ...), custom_call_target="tpu_custom_call" | custom-call | tf_op jit(solution)/shard_map/finish/pallas_call | solution.py:708
  121.2 1.3 %slice_bitcast_fusion = f32[1,16,32]{2,1,0:T(8,128)} fusion(f32[34,128]{1,0:T(8,128)} %finish.1), kind=kLoop, calls=%fused_computation.1 | loop fusion | bytes 4096 | tf_op jit(solution)/shard_map/broadcast_in_dim | solution.py:745
  122.5 1.2 slice.9
  123.7 1.3 %slice.11 = f32[1,16]{1,0:T(1,128)} slice(f32[34,128]{1,0:T(8,128)} %finish.1), slice={[16:17], [32:48]} | slice | bytes 128 | tf_op jit(solution)/shard_map/slice | solution.py:745
  (1 shorter events, 0.0 us)
Async XLA Ops:
  2.4 1.6 %copy-start.1 = (bf16[1,32,32768]{2,1,0:T(8,128)(2,1)S(1)}, bf16[1,32,32768]{2,1,0:T(8,128)(2,1)}, u32[]{:S(2)}) copy-start(bf16[1,32,32768]{2,1,0:T(8,128)(2,1)} %param.11) | copy-start | bytes 6291460
  4.0 87.7 %copy-start.3 = (bf16[1,16]{1,0:T(2,128)(2,1)S(1)}, bf16[1,16]{1,0:T(2,128)(2,1)}, u32[]{:S(2)}) copy-start(bf16[1,16]{1,0:T(2,128)(2,1)} %prop_out_ref.1) | copy-start | bytes 100
  22.0 3.2 %copy-start = (bf16[32768,128]{1,0:T(8,128)(2,1)}, bf16[32768,128]{1,0:T(8,128)(2,1)S(1)}, u32[]{:S(2)}) copy-start(bf16[32768,128]{1,0:T(8,128)(2,1)S(1)} %get-tuple-element.9.table_hbm) | copy-start | bytes 25165828
  25.2 1.0 copy-start.2

commit v6 on v5

--- a/solution.py
+++ b/solution.py
@@ -66,7 +66,6 @@
         return carry
 
     lax.fori_loop(1, sources, greet, 0)
-    pl.semaphore_wait(barrier, sources - 1)
 
     def copy(step):
         peer = lax.rem(me + step, sources)
@@ -87,7 +86,6 @@
         copy(step).wait()
         return carry
 
-    lax.fori_loop(1, sources, start, 0)
     own = pltpu.make_async_copy(geom_ref.at[me], arrived.at[me], local.at[PIECES])
     own.start()
 
@@ -115,6 +113,9 @@
             piece * per_piece, (piece + 1) * per_piece, build, state, unroll=4
         )
         table_piece(table, table_hbm, local, piece).start()
+        if piece == 0:
+            pl.semaphore_wait(barrier, sources - 1)
+            lax.fori_loop(1, sources, start, 0)
     own.wait()
     lax.fori_loop(1, sources, finish, 0)
     geo_ref[...] = arrived[...].astype(f32)
@@ -141,7 +142,7 @@
     for piece in range(PIECES):
         table_piece(table_hbm, narrow, kept_sems, piece).start()
 
-    hidden = fine_in_ref.shape[0]
+    hidden = fine_in_ref.shape[1]
     groups = TILE // PART
 
     def diagonal(weights):
@@ -160,7 +161,9 @@
         column = lax.broadcasted_iota(jnp.int32, tall.shape, 1) // columns
         return jnp.where(row == column, tall, 0.0).astype(bf16)
 
-    first_all[pl.ds(0, groups * hidden), :] = diagonal(fine_in_ref[...]).astype(bf16)
+    first_all[pl.ds(0, groups * hidden), :] = diagonal(
+        jnp.transpose(fine_in_ref[...].astype(f32))
+    ).astype(bf16)
     first_all[pl.ds(groups * hidden, groups * 16), :] = diagonal(prop_in_ref[...]).astype(bf16)
     for layer in range(fine_mid_ref.shape[0]):
         mid_all[layer] = diagonal(fine_mid_ref[layer]).astype(bf16)
@@ -407,7 +410,6 @@
     for step in range(1, replicas):
         other = lax.rem(replica + step, replicas)
         pl.semaphore_signal(barrier, inc=1, device_id=(me, other), device_id_type=MESH)
-    pl.semaphore_wait(barrier, sources + replicas - 2)
 
     def exchange(source, target, send, recv):
         def copy(step):
@@ -432,9 +434,6 @@
         lax.fori_loop(1, sources, start, 0)
         return lambda: lax.fori_loop(1, sources, finish, 0)
 
-    wait_stats = exchange(stats_ref, stats_in, stats_send, stats_recv)
-    own_stats = pltpu.make_async_copy(stats_ref.at[me], stats_in.at[me], local.at[2])
-    own_stats.start()
 
     part_row = lax.broadcasted_iota(jnp.int32, (sources, 128), 0)
     group = lax.broadcasted_iota(jnp.int32, (sources, 128), 1) // 32
@@ -455,8 +454,10 @@
     def exact(first, second):
         return jnp.dot(first, second, precision=lax.Precision.HIGHEST, preferred_element_type=f32)
 
-    def dense(seated):
-        return exact(fold, jnp.where(group == seat, seated, 0.0))
+    def dense(*seated):
+        masked = [jnp.where(group == seat, value, 0.0) for value in seated]
+        folded = exact(fold, jnp.concatenate(masked, axis=1))
+        return [folded[:, i * 128 : (i + 1) * 128] for i in range(len(seated))]
 
     def four(value):
         return jnp.concatenate([value] * 4, axis=1)
@@ -475,12 +476,20 @@
     )
     count_column = jnp.sum(jnp.where(diagonal, counts, 0.0), axis=1, keepdims=True)
     slot_lane = (lax.broadcasted_iota(jnp.int32, (sources, 128), 1) % 32).astype(f32)
-    live = as_row(dense(jnp.where(slot_lane < count_column, 1.0, 0.0)))
-    rays = dense(four(ray_ref[...].astype(f32)))
-    ranks = dense(four(rank_ref[...].astype(f32)))
+    live, rays, ranks = dense(
+        jnp.where(slot_lane < count_column, 1.0, 0.0),
+        four(ray_ref[...].astype(f32)),
+        four(rank_ref[...].astype(f32)),
+    )
+    live = as_row(live)
     keys = rays * 64.0 + ranks
     key_row, rank_row = as_row(keys), as_row(ranks)
     key_column, ray_column = jnp.transpose(keys), jnp.transpose(rays)
+    pl.semaphore_wait(barrier, sources + replicas - 2)
+    wait_stats = exchange(stats_ref, stats_in, stats_send, stats_recv)
+    own_stats = pltpu.make_async_copy(stats_ref.at[me], stats_in.at[me], local.at[2])
+    own_stats.start()
+
     for chunk in range(blocks):
         gap = key_row - key_column[:, chunk : chunk + 1]
         ahead[pl.ds(chunk * 128, 128), :] = jnp.where(
@@ -499,12 +508,13 @@
         value = turned[(3 - index) % 4]
         for place in range(3):
             value = jnp.where(seat == place, turned[(place - index) % 4], value)
-        return as_row(dense(value))
-
-    sum_aa, sum_ab, sum_bb, log_prop = (stat(index) for index in range(4))
+        return value
+
     for index in range(sources):
         flat[pl.ds(index, 1), :] = stats_in[index, pl.ds(1, 1), :]
-    log_fine = as_row(dense(flat[...]))
+    sum_aa, sum_ab, sum_bb, log_prop, log_fine = (
+        as_row(value) for value in dense(*(stat(index) for index in range(4)), flat[...])
+    )
 
     def stacked(values):
         pieces = [piece.astype(f32) for value in values for piece in split_three(value)]
@@ -525,8 +535,9 @@
         (carried[0:1] + carried[1:2] + carried[2:3]) * live,
     )
     message = jnp.zeros((sources, 128), f32)
-    for index, value in enumerate(outgoing):
-        spread = exact(unfold, as_dense(value))
+    spreads = exact(unfold, jnp.concatenate([as_dense(value) for value in outgoing], axis=1))
+    for index in range(len(outgoing)):
+        spread = spreads[:, index * 128 : (index + 1) * 128]
         for place in range(4):
             shift = 32 * ((index - place) % 4)
             moved = pltpu.roll(spread, shift, 1) if shift else spread
@@ -609,8 +620,19 @@
     summed = grads_in[0]
     for index in range(1, replicas):
         summed = summed + grads_in[index]
-    result_ref[pl.ds(0, 16), :] = summed[0:16] * prop_out_ref[...]
+    head = jnp.broadcast_to(prop_out_ref[...].astype(f32), (16, 16))
+    on_diagonal = lax.broadcasted_iota(jnp.int32, (16, 16), 0) == lax.broadcasted_iota(
+        jnp.int32, (16, 16), 1
+    )
+    head_column = jnp.sum(jnp.where(on_diagonal, head, 0.0), axis=1, keepdims=True)
+    result_ref[pl.ds(0, 16), :] = summed[0:16] * head_column
     result_ref[pl.ds(16, 16), :] = summed[16:32]
+
+
+def split_kernel(result_ref, loss_ref, in_ref, out_ref):
+    loss_ref[...] = result_ref[pl.ds(32, RAY_DEV // 128), :]
+    in_ref[...] = result_ref[pl.ds(0, 16), :][:, 0:32]
+    out_ref[...] = result_ref[pl.ds(16, 1), :][:, 32:48]
 
 
 def vmem():
@@ -659,7 +681,7 @@
             pltpu.SemaphoreType.DMA((PIECES + 1,)),
         ],
         compiler_params=pltpu.CompilerParams(
-            vmem_limit_bytes=40 * 2**20, collective_id=1, has_side_effects=True
+            vmem_limit_bytes=60 * 2**20, collective_id=1, has_side_effects=True
         ),
         name="scatter_geometry",
     )(by_part, feature_grid[0])
@@ -699,7 +721,7 @@
         (sample_cells * 2).reshape(sources * width),
         geometry,
         corners,
-        fine_in[0],
+        jnp.swapaxes(fine_in, 1, 2)[0],
         fine_mid[0],
         fine_out,
         prop_in[0],
@@ -738,11 +760,22 @@
         slot_ray[0, 0],
         slot_rank[0, 0],
         bucket_count[0],
-        prop_out[0].astype(f32)[:, None],
+        prop_out,
         back,
         kept,
     )
-    return (result[32:].reshape(1, 1, RAY_DEV), result[None, 0:16, 0:32], result[16:17, 32:48])
+    ray_loss, in_grad, out_grad = pl.pallas_call(
+        split_kernel,
+        out_shape=(
+            jax.ShapeDtypeStruct((RAY_DEV // 128, 128), f32),
+            jax.ShapeDtypeStruct((16, 32), f32),
+            jax.ShapeDtypeStruct((1, 16), f32),
+        ),
+        in_specs=[vmem()],
+        out_specs=(vmem(), vmem(), vmem()),
+        name="split",
+    )(result)
+    return (ray_loss.reshape(1, 1, RAY_DEV), in_grad[None], out_grad)
 
 
 def solution(mesh):

time: 126 us -> 118 us (0.937)
  local copies, waits for them, and re-layouts: 14.2 us -> 3.37 us
  Pallas kernels: 109 us -> 112 us
    unnamed x10 -> x1, local copies, waits for them, and re-layouts: 7.93 us -> 0.74 us
    slice x2 -> x0, local copies, waits for them, and re-layouts: 2.51 us -> none  [the longest x1 1.26 us: on_device(): result[16:17, 32:48]]
    pallas_call x0 -> x1, Pallas kernels: none -> 1.33 us  [on_device(): pl.pallas_call(split_kernel, out_shape=(jax.ShapeDtypeStruct((RAY_DEV //...]
    broadcast_in_dim x1 -> x0, local copies, waits for them, and re-layouts: 1.3 us -> none  [on_device(): result[None, 0:16, 0:32]]
where the time goes in v6:
time: 118 us; the launch traced here: 117 us
  Pallas kernels  112 us (95%)
  local copies, waits for them, and re-layouts  3.37 us (3%)
    pallas_call x1, Pallas kernels, on_device(): pl.pallas_call(owner_kernel, out_shape=(jax.ShapeDtypeStruct((sources, 48...  62.5 us
    pallas_call x1, Pallas kernels, on_device(): pl.pallas_call(finish_kernel, out_shape=jax.ShapeDtypeStruct((32 + RAY_DE...  29.7 us
    pallas_call x1, Pallas kernels, on_device(): pl.pallas_call(scatter_kernel, out_shape=(jax.ShapeDtypeStruct(by_part.sh...  18.4 us

profile of v6, /device:TPU:0, one launch (start us, length us, event | category | flops | bytes accessed | tf_op | source)
XLA Modules:
  0.0 116.9 jit_solution(14206146622061091248)
XLA Ops:
  0.6 1.0 multiply_bitcast_fusion
  1.6 0.7 copy.15
  2.3 1.4 %copy.14 = bf16[32,4,2048]{2,1,0:T(4,128)(2,1)S(1)} copy(bf16[32,4,2048]{2,0,1:T(8,128)(2,1)} %bitcast.19) | data formatting | bytes 1048576 | tf_op jit(solution)/shard_map/transpose | solution.py:665
  3.8 1.2 %reshape.20.geom_ref = bf16[32,64,128]{2,1,0:T(8,128)(2,1)} reshape(bf16[32,4,2048]{2,1,0:T(4,128)(2,1)S(1)} %copy.14) | data formatting | bytes 1048576 | tf_op jit(solution)/shard_map/reshape | solution.py:666
  5.0 18.4 %scatter_geometry.1 = (f32[32,64,128]{2,1,0:T(8,128)}, bf16[32768,128]{1,0:T(8,128)(2,1)}) custom-call(bf16[32,64,128]{2,1,0:T(8,128)(2,1)} %reshape.20.geom_ref, bf16[32,32768]{1,0:T(8,128)(2,1)} %bitcast.17), custom_call_target="tpu_custom_call" | custom-call | tf_op jit(solution)/shard_map/scatter_geometry/pallas_call | solution.py:668
  23.4 62.5 %owner_forward.1 = (bf16[32,48,2048]{2,1,0:T(8,128)(2,1)}, f32[4,512,128]{2,1,0:T(8,128)}, f32[32,2,128]{2,1,0:T(2,128)}) custom-call(s32[65536]{0:T(1024)} %bitcast.18, f32[32,64,128]{2,1,0:T(8,128)} %get-tuple-element.11.geo, bf16[32768,128]{1,0:T(8,128)(2,1)} %get-tuple-element.12.table_hbm, bf16[32,64]{1,0:T(8,128)(2,1)} %bitcast.23, ...), custom_call_target="tpu_custom_call" | custom-call | tf_op jit(solution)/shard_map/owner_forward/pallas_call | solution.py:688
  85.9 29.7 %finish.1.result_ref = f32[34,128]{1,0:T(8,128)} custom-call(f32[32,2,128]{2,1,0:T(2,128)} %get-tuple-element.13.stats_ref, s32[32,32]{1,0:T(8,128)} %bitcast.21, s32[32,32]{1,0:T(8,128)} %bitcast.22, s32[1,32]{1,0:T(1,128)} %bitcast.25, bf16[1,16]{1,0:T(2,128)(2,1)} %prop_out_ref.3, f32[4,512,128]{2,1,0:T(8,128)} %get-tuple-element.14.back_hbm, ...), custom_call_target="tpu_custom_call" | custom-call | tf_op jit(solution)/shard_map/finish/pallas_call | solution.py:730
  115.6 1.3 %split.1 = (f32[2,128]{1,0:T(2,128)}, f32[16,32]{1,0:T(8,128)}, f32[1,16]{1,0:T(1,128)}) custom-call(f32[34,128]{1,0:T(8,128)} %finish.1.result_ref), custom_call_target="tpu_custom_call" | custom-call | tf_op jit(solution)/shard_map/split/pallas_call | solution.py:767

commit v7 on v6

--- a/solution.py
+++ b/solution.py
@@ -9,10 +9,10 @@
 
 GR = 32
 RAY_DEV = 256
-TILE = 1024
+TILE = 2048
 PIECES = 4
-PART = 256
-SHARES = (0, 128, 384, 640, 896, 1024)
+PART = 512
+SHARES = (0, 256, 768, 1280, 1792, 2048)
 
 distill_weight = 50.0
 f32 = jnp.float32
@@ -299,9 +299,9 @@
         ahead = networks(jnp.maximum(tile - 1, 0), hold_last)
         now = interpolate(tile, out_of, hold_now)
         for slot in range(slots):
+            next(now, None)
             gather(indices, into, SHARES[slot], SHARES[slot + 1])
             next(ahead, None)
-            next(now, None)
         for unused in ahead:
             pass
 
@@ -311,9 +311,9 @@
     gather(even_cells, even)
 
     def step(tile, carry):
-        @pl.when((tile % 2 == 0) & (tile >= 4))
+        @pl.when(tile >= 2)
         def _():
-            save(tile // 2 - 2).start()
+            save(tile - 2).start()
 
         @pl.when(tile % 2 == 0)
         def _():

time: 118 us -> 115 us (0.975)
  Pallas kernels: 112 us -> 110 us
    pallas_call x1, Pallas kernels: 62.5 us -> 60.2 us  [on_device(): pl.pallas_call(owner_kernel, out_shape=(jax.ShapeDtypeStruct((sources, 48...]
where the time goes in v7:
time: 115 us
  Pallas kernels  110 us (96%)
  local copies, waits for them, and re-layouts  3.37 us (3%)
    pallas_call x1, Pallas kernels, on_device(): pl.pallas_call(owner_kernel, out_shape=(jax.ShapeDtypeStruct((sources, 48...  60.2 us
    pallas_call x1, Pallas kernels, on_device(): pl.pallas_call(finish_kernel, out_shape=jax.ShapeDtypeStruct((32 + RAY_DE...  29.7 us
    pallas_call x1, Pallas kernels, on_device(): pl.pallas_call(scatter_kernel, out_shape=(jax.ShapeDtypeStruct(by_part.sh...  18.4 us

profile of v7, /device:TPU:0, one launch (start us, length us, event | category | flops | bytes accessed | tf_op | source)
XLA Modules:
  0.0 114.7 jit_solution(4656774692219472023)
XLA Ops:
  0.6 1.0 multiply_bitcast_fusion
  1.6 0.7 copy.15
  2.3 1.4 %copy.14 = bf16[32,4,2048]{2,1,0:T(4,128)(2,1)S(1)} copy(bf16[32,4,2048]{2,0,1:T(8,128)(2,1)} %bitcast.19) | data formatting | bytes 1048576 | tf_op jit(solution)/shard_map/transpose | solution.py:665
  3.8 1.2 %reshape.20.geom_ref = bf16[32,64,128]{2,1,0:T(8,128)(2,1)} reshape(bf16[32,4,2048]{2,1,0:T(4,128)(2,1)S(1)} %copy.14) | data formatting | bytes 1048576 | tf_op jit(solution)/shard_map/reshape | solution.py:666
  5.0 18.4 %scatter_geometry.1 = (f32[32,64,128]{2,1,0:T(8,128)}, bf16[32768,128]{1,0:T(8,128)(2,1)}) custom-call(bf16[32,64,128]{2,1,0:T(8,128)(2,1)} %reshape.20.geom_ref, bf16[32,32768]{1,0:T(8,128)(2,1)} %bitcast.17), custom_call_target="tpu_custom_call" | custom-call | tf_op jit(solution)/shard_map/scatter_geometry/pallas_call | solution.py:668
  23.4 60.2 %owner_forward.1 = (bf16[32,48,2048]{2,1,0:T(8,128)(2,1)}, f32[4,512,128]{2,1,0:T(8,128)}, f32[32,2,128]{2,1,0:T(2,128)}) custom-call(s32[65536]{0:T(1024)} %bitcast.18, f32[32,64,128]{2,1,0:T(8,128)} %get-tuple-element.11.geo, bf16[32768,128]{1,0:T(8,128)(2,1)} %get-tuple-element.12.table_hbm, bf16[32,64]{1,0:T(8,128)(2,1)} %bitcast.23, ...), custom_call_target="tpu_custom_call" | custom-call | tf_op jit(solution)/shard_map/owner_forward/pallas_call | solution.py:688
  83.7 29.7 %finish.1.result_ref = f32[34,128]{1,0:T(8,128)} custom-call(f32[32,2,128]{2,1,0:T(2,128)} %get-tuple-element.13.stats_ref, s32[32,32]{1,0:T(8,128)} %bitcast.21, s32[32,32]{1,0:T(8,128)} %bitcast.22, s32[1,32]{1,0:T(1,128)} %bitcast.25, bf16[1,16]{1,0:T(2,128)(2,1)} %prop_out_ref.3, f32[4,512,128]{2,1,0:T(8,128)} %get-tuple-element.14.back_hbm, ...), custom_call_target="tpu_custom_call" | custom-call | tf_op jit(solution)/shard_map/finish/pallas_call | solution.py:730
  113.4 1.3 %split.1 = (f32[2,128]{1,0:T(2,128)}, f32[16,32]{1,0:T(8,128)}, f32[1,16]{1,0:T(1,128)}) custom-call(f32[34,128]{1,0:T(8,128)} %finish.1.result_ref), custom_call_target="tpu_custom_call" | custom-call | tf_op jit(solution)/shard_map/split/pallas_call | solution.py:767
